TPU v7x, 32 devices: a whole 2x2x4 slice. The times are simulated.
32 devices in a mesh: dp: 4 (over y, core), mp: 8 (over z, x).
Axes of the slice: x: 2, y: 2, z: 4, core: 2. Of those that a mesh axis runs over, the one named last changes fastest.
Arguments:
- prediction_maps: bfloat16 [4, 72, 384, 768], P('dp', None, 'mp'), may hold values from -6 to 6
- observed_maps: bfloat16 [4, 72, 384, 768], P('dp', None, 'mp'), may hold values from -6 to 6
- zonal_wavenumber_map: int32 [384], P('mp'), may hold values from 0 to 383, as said below
- associated_function_table: bfloat16 [384, 384, 384], P('mp', 'dp'), as said below
- magnitude_factor: float32 [384, 72], replicated, may hold values from 1 to 10
- phase_match_factor: float32 [384, 72], replicated, may hold values from 0.1 to 1
Outputs:
- grad_forecast: bfloat16 [4, 72, 384, 768], P('dp', None, 'mp')
Inputs may be any that keep to these rules, and one draw needn't show every extreme that they name: `zonal_wavenumber_map`: slots stand 48 to an index of mp in order; each order appears in exactly one slot; in every index's block the first half holds orders below 192 and the second half orders of 192 or more. associated_function_table[s, q, l] is zero wherever l is below zonal_wavenumber_map[s].
All inputs are finite; a program needn't handle non-finite values.
Results may differ from a plain program's by a relative error of at most 0.008.
Values may be sent and summed in bfloat16 or wider, within the bound.
A program may use at most 192 MiB of HBM per device.

v0:
```python
import math

import jax
import jax.numpy as jnp
from jax import lax
from jax.sharding import PartitionSpec as P

MERIDIAN_POINTS = 768


def transform_table(orders):
    longitude = jnp.arange(MERIDIAN_POINTS, dtype=jnp.int32)
    phase_index = longitude[:, None] * orders[None, :] % MERIDIAN_POINTS
    radians = phase_index.astype(jnp.float32) * (2.0 * math.pi / MERIDIAN_POINTS)
    norm_factor = 1.0 / math.sqrt(MERIDIAN_POINTS)
    return jnp.stack(
        [jnp.cos(radians) * norm_factor, -jnp.sin(radians) * norm_factor], axis=1
    ).astype(jnp.bfloat16)


def local(
    prediction_maps,
    observed_maps,
    zonal_wavenumber_map,
    associated_function_table,
    magnitude_factor,
    phase_match_factor,
):
    orders = lax.all_gather(zonal_wavenumber_map, "mp", axis=0, tiled=True)
    fourier = transform_table(orders)
    estimate_surface = prediction_maps[0]
    grid_true = observed_maps[0]
    channels = estimate_surface.shape[0]
    lat_dev = estimate_surface.shape[1]
    degrees = associated_function_table.shape[2]
    slot_count = zonal_wavenumber_map.shape[0]
    half_slots = slot_count // 2
    coeff_width = 2 * channels
    spec_pred = jnp.einsum(
        "cqo,okm->mqkc", estimate_surface, fourier, preferred_element_type=jnp.float32
    )
    spec_pred = spec_pred.reshape(degrees, lat_dev, coeff_width).astype(jnp.bfloat16)
    spec_true = jnp.einsum("cqo,okm->mqkc", grid_true, fourier, preferred_element_type=jnp.float32)
    spec_true = spec_true.reshape(degrees, lat_dev, coeff_width).astype(jnp.bfloat16)
    local_pred, local_true = (
        lax.all_to_all(spec_pred, "mp", split_axis=0, concat_axis=1, tiled=True),
        lax.all_to_all(spec_true, "mp", split_axis=0, concat_axis=1, tiled=True),
    )
    skipped = 0
    full_table = lax.all_gather(associated_function_table, "dp", axis=1, tiled=True)
    table_low = full_table[:half_slots]
    table_high = full_table[half_slots:, :, skipped:]
    low_pred = jnp.einsum(
        "sql,sqk->slk", table_low, local_pred[:half_slots], preferred_element_type=jnp.float32
    )
    low_true = jnp.einsum(
        "sql,sqk->slk", table_low, local_true[:half_slots], preferred_element_type=jnp.float32
    )
    high_pred = jnp.einsum(
        "sql,sqk->slk", table_high, local_pred[half_slots:], preferred_element_type=jnp.float32
    )
    high_true = jnp.einsum(
        "sql,sqk->slk", table_high, local_true[half_slots:], preferred_element_type=jnp.float32
    )
    order_weight = jnp.where(zonal_wavenumber_map == 0, 1.0, 2.0).astype(jnp.float32)

    def order_power(harmonic_expansion, weights):
        quadratic_terms = (
            harmonic_expansion[..., :channels] ** 2 + harmonic_expansion[..., channels:] ** 2
        )
        return jnp.sum(weights[:, None, None] * quadratic_terms, axis=0)

    part_pred = order_power(low_pred, order_weight[:half_slots]) + order_power(
        high_pred, order_weight[half_slots:]
    )
    part_true = order_power(low_true, order_weight[:half_slots]) + order_power(
        high_true, order_weight[half_slots:]
    )
    pred_power, true_power = lax.psum((part_pred, part_true), "mp")
    power_ratio = jnp.sqrt((true_power + 1.0) / (pred_power + 1.0))
    pred_factor = (
        2.0 * magnitude_factor * (1.0 - power_ratio) + 2.0 * phase_match_factor * power_ratio
    )
    true_factor = -2.0 * phase_match_factor
    pred_wide = jnp.concatenate([pred_factor, pred_factor], axis=1)
    true_wide = jnp.concatenate([true_factor, true_factor], axis=1)
    low_weight = order_weight[:half_slots, None, None]
    high_weight = order_weight[half_slots:, None, None]
    grad_low = (low_weight * (pred_wide * low_pred + true_wide * low_true)).astype(jnp.bfloat16)
    grad_high = (high_weight * (pred_wide * high_pred + true_wide * high_true)).astype(jnp.bfloat16)
    low_part = jnp.einsum(
        "sql,slk->sqk", full_table[:half_slots], grad_low, preferred_element_type=jnp.float32
    )
    high_part = jnp.einsum(
        "sql,slk->sqk",
        full_table[half_slots:, :, skipped:],
        grad_high,
        preferred_element_type=jnp.float32,
    )
    spectral_sensitivity = jnp.concatenate([low_part, high_part], axis=0)
    spectral_sensitivity = spectral_sensitivity.astype(jnp.bfloat16)
    grad_lat = lax.all_to_all(spectral_sensitivity, "mp", split_axis=1, concat_axis=0, tiled=True)
    grad_lat = grad_lat.reshape(degrees, lat_dev, 2, channels)
    grad_grid = jnp.einsum("okm,mqkc->cqo", fourier, grad_lat, preferred_element_type=jnp.float32)
    return grad_grid.astype(jnp.bfloat16)[None]


def solution(mesh):
    return jax.shard_map(
        local,
        mesh=mesh,
        in_specs=(
            P("dp", None, "mp", None),
            P("dp", None, "mp", None),
            P("mp"),
            P("mp", "dp", None),
            P(),
            P(),
        ),
        out_specs=P("dp", None, "mp", None),
        check_vma=False,
    )
```

profile of v0, /device:TPU:0, one launch (start us, length us, event | category | flops | bytes accessed | tf_op | source)
XLA Modules:
  0.0 897.1 jit_solution(3180946542927738272)
XLA Ops:
  6.5 0.0 all-gather.2.cloned.1.call-start
  6.5 0.7 all-gather.2.cloned.1.call-update
  7.3 1.2 dynamic-slice
  9.2 0.9 dynamic-update-slice
  10.0 13.1 %all-reduce = s32[384]{0:T(512)S(1)} all-reduce(s32[384]{0:T(512)S(1)} %dynamic-update-slice), channel_id=1, replica_groups=mesh['dp'=4,'mp'=8] {'mp'}, use_global_device_ids=true, to_apply=%add | all-reduce | flops 384 | bytes 3072
  23.1 5.1 multiply_convert_fusion.9
  28.1 0.0 copy-start.1
  28.2 0.0 copy-start.3
  28.2 9.8 %convert_bitcast_fusion.1 = bf16[384,48,2,72]{0,3,1,2:T(8,128)(2,1)S(1)} fusion(bf16[72,48,768]{2,1,0:T(8,128)(2,1)} %bitcast.80, bf16[768,1,384]{2,0,1:T(8,128)(2,1)S(1)} %get-tuple-element.18, bf16[768,1,384]{2,0,1:T(8,128)(2,1)S(1)} %get-tuple-element.17), kind=kOutput, calls=%fused_computation.24 | convolution fusion | flops 4081876992 | bytes 11796480 | tf_op jit(solution)/shard_map/cqo,okm->mqkc/dot_general | solution.py:43
  38.0 2.9 copy.30
  40.9 13.3 %copy.31 = bf16[384,48,144]{2,1,0:T(8,128)(2,1)} copy(bf16[384,48,144]{0,2,1:T(8,128)(2,1)} %bitcast.72) | data formatting | bytes 10616832 | tf_op jit(solution)/shard_map/convert_element_type | solution.py:44
  54.2 5.0 all-to-all-start
  59.2 0.0 copy-done.1
  59.3 0.0 copy-done.3
  59.3 9.4 %convert_bitcast_fusion = bf16[384,48,2,72]{0,3,1,2:T(8,128)(2,1)S(1)} fusion(bf16[72,48,768]{2,1,0:T(8,128)(2,1)} %bitcast.81, bf16[768,1,384]{2,0,1:T(8,128)(2,1)S(1)} %get-tuple-element.18, bf16[768,1,384]{2,0,1:T(8,128)(2,1)S(1)} %get-tuple-element.17), kind=kOutput, calls=%fused_computation.23 | convolution fusion | flops 4081876992 | bytes 11796480 | tf_op jit(solution)/shard_map/cqo,okm->mqkc/dot_general | solution.py:39
  68.7 2.9 copy.37
  71.6 13.2 %copy.38 = bf16[384,48,144]{2,1,0:T(8,128)(2,1)} copy(bf16[384,48,144]{0,2,1:T(8,128)(2,1)} %bitcast.73) | data formatting | bytes 10616832 | tf_op jit(solution)/shard_map/convert_element_type | solution.py:42
  84.8 0.0 copy-start.7
  84.8 178.2 %all-to-all-done = bf16[384,48,144]{2,1,0:T(8,128)(2,1)} async-done(((bf16[384,48,144]{2,1,0:T(8,128)(2,1)}), bf16[384,48,144]{2,1,0:T(8,128)(2,1)}, u32[]{:S(2)}, u32[]{:S(2)}) %all-to-all-start) | async-done | bytes 5308448 | tf_op jit(solution)/shard_map/all_to_all | solution.py:47
  263.0 5.1 all-to-all-start.1
  268.1 0.2 all-reduce.4.cloned.1.call-start
  268.3 0.0 copy-done.7
  268.4 0.1 fusion.70
  268.4 6.6 fusion.69
  275.0 2.7 copy.34
  277.7 194.7 %all-to-all-done.1 = bf16[384,48,144]{2,1,0:T(8,128)(2,1)} async-done(((bf16[384,48,144]{2,1,0:T(8,128)(2,1)}), bf16[384,48,144]{2,1,0:T(8,128)(2,1)}, u32[]{:S(2)}, u32[]{:S(2)}) %all-to-all-start.1) | async-done | bytes 5308448 | tf_op jit(solution)/shard_map/all_to_all | solution.py:46
  472.5 4.4 fusion.68
  476.9 2.6 copy.41
  479.5 0.0 slice-start
  479.5 0.0 slice-start.1
  479.5 2.9 copy.39
  482.4 1.0 slice-done
  483.4 0.1 slice-done.1
  483.5 2.6 copy.32
  486.1 0.0 all-gather.2.cloned.1.call-done
  486.1 0.0 copy-start
  486.1 9.3 %fusion.47 = f32[24,384,144]{1,2,0:T(8,128)} fusion(bf16[24,384,144]{2,1,0:T(8,128)(2,1)} %bitcast.74, bf16[48,384,384]{2,1,0:T(8,128)(2,1)} %all-gather.2.cloned.1.call-done), kind=kOutput, calls=%fused_computation.55 | convolution fusion | flops 1019215872 | bytes 17104896 | tf_op jit(solution)/shard_map/sql,sqk->slk/dot_general | solution.py:62
  495.4 1.1 copy-done
  496.5 6.7 fusion.50
  503.2 6.7 fusion.44
  509.9 6.8 fusion.41
  516.7 0.0 copy-start.5
  516.7 0.0 copy-start.6
  516.7 8.3 fusion.31
  525.0 0.7 add.61
  525.7 0.7 add.57
  526.3 0.0 all-reduce.4.cloned.1.call-update
  526.3 70.0 %all-reduce.4.cloned.1.call-done = (f32[384,72]{0,1:T(8,128)}, f32[384,72]{0,1:T(8,128)}) async-done(((f32[384,72]{0,1:T(8,128)}, f32[384,72]{0,1:T(8,128)}), (f32[384,72]{0,1:T(8,128)}, f32[384,72]{0,1:T(8,128)})) %all-reduce.4.cloned.1.call-update) | async-done | bytes 221200 | tf_op jit(solution)/shard_map/psum | solution.py:79
  596.4 0.0 copy-done.5
  596.4 0.0 copy-done.6
  596.4 1.0 multiply_add_fusion
  597.5 8.8 convert_bitcast_fusion.2
  606.3 10.3 %convert_bitcast_fusion.3 = bf16[24,384,144]{1,2,0:T(8,128)(2,1)} fusion(bf16[48,384,384]{2,1,0:T(8,128)(2,1)} %all-gather.2.cloned.1.call-done, f32[24,384,144]{1,2,0:T(8,128)} %fusion.41, f32[24,384,144]{1,2,0:T(8,128)} %fusion.44, f32[384,144]{0,1:T(8,128)S(1)} %pad_maximum_fusion.6, f32[384,144]{0,1:T(8,128)S(1)} %pad_maximum_fusion.5, ...), kind=kOutput, calls=%fused_computation.47 | convolution fusion | flops 1027178496 | bytes 20791392 | tf_op jit(solution)/shard_map/sql,slk->sqk/dot_general | solution.py:91
  616.6 4.7 pad_maximum_fusion
  621.3 13.2 %copy.43 = bf16[48,384,144]{2,0,1:T(8,128)(2,1)} copy(bf16[48,384,144]{1,2,0:T(8,128)(2,1)} %pad_maximum_fusion) | data formatting | bytes 10616832 | tf_op jit(solution)/shard_map/concatenate | solution.py:100
  634.5 210.1 %all_to_all.45 = bf16[48,384,144]{2,0,1:T(8,128)(2,1)} all-to-all(bf16[48,384,144]{2,0,1:T(8,128)(2,1)} %copy.43), channel_id=1, replica_groups=mesh['dp'=4,'mp'=8] {'mp'}, dimensions={1} | all-to-all | bytes 10616832 | tf_op jit(solution)/shard_map/all_to_all | solution.py:102
  844.6 16.0 %copy.55 = bf16[8,48,48,144]{1,0,3,2:T(8,128)(2,1)} copy(bf16[8,48,48,144]{3,1,2,0:T(8,128)(2,1)} %bitcast.71) | data formatting | bytes 10616832 | tf_op jit(solution)/shard_map/reshape | solution.py:103
  860.6 0.0 copy-start.2
  860.6 0.0 copy-start.4
  860.6 18.8 %reshape.111 = bf16[384,48,2,72]{0,3,2,1:T(8,128)(2,1)} reshape(bf16[8,48,48,144]{1,0,3,2:T(8,128)(2,1)} %copy.55) | data formatting | bytes 10616832 | tf_op jit(solution)/shard_map/reshape | solution.py:103
  879.5 0.0 copy-done.2
  879.5 0.0 copy-done.4
  879.5 7.4 fusion.12
  886.8 3.4 copy.47
  (5 shorter events, 0.0 us)
Async XLA Ops:
  6.5 479.6 %all-gather.2.cloned.1.call-start = ((), (), s32[]{:S(2)}) async-start(), calls=%async_computation.3 | async-start | bytes 17694720 | tf_op jit(solution)/shard_map/all_gather | solution.py:50
  28.1 31.1 %copy-start.1 = (bf16[768,1,384]{2,0,1:T(8,128)(2,1)}, bf16[768,1,384]{2,0,1:T(8,128)(2,1)S(1)}, u32[]{:S(2)}) copy-start(bf16[768,1,384]{2,0,1:T(8,128)(2,1)S(1)} %get-tuple-element.17) | copy-start | bytes 1769476
  28.2 31.1 %copy-start.3 = (bf16[768,1,384]{2,0,1:T(8,128)(2,1)}, bf16[768,1,384]{2,0,1:T(8,128)(2,1)S(1)}, u32[]{:S(2)}) copy-start(bf16[768,1,384]{2,0,1:T(8,128)(2,1)S(1)} %get-tuple-element.18) | copy-start | bytes 1769476
  54.2 208.8 %all-to-all-start = ((bf16[384,48,144]{2,1,0:T(8,128)(2,1)}), bf16[384,48,144]{2,1,0:T(8,128)(2,1)}, u32[]{:S(2)}, u32[]{:S(2)}) async-start(bf16[384,48,144]{2,1,0:T(8,128)(2,1)} %copy.31), calls=%async_computation | async-start | bytes 18874368 | tf_op jit(solution)/shard_map/all_to_all | solution.py:47
  84.8 183.5 %copy-start.7 = (s32[48]{0:T(128)S(1)}, s32[48]{0:T(128)}, u32[]{:S(2)}) copy-start(s32[48]{0:T(128)} %param.8) | copy-start | bytes 580
  263.0 209.4 %all-to-all-start.1 = ((bf16[384,48,144]{2,1,0:T(8,128)(2,1)}), bf16[384,48,144]{2,1,0:T(8,128)(2,1)}, u32[]{:S(2)}, u32[]{:S(2)}) async-start(bf16[384,48,144]{2,1,0:T(8,128)(2,1)} %copy.38), calls=%async_computation.1 | async-start | bytes 18874368 | tf_op jit(solution)/shard_map/all_to_all | solution.py:46
  268.1 328.3 %all-reduce.4.cloned.1.call-start = ((), (), s32[]{:S(2)}) async-start(), calls=%async_computation.4 | async-start | bytes 442368 | tf_op jit(solution)/shard_map/psum | solution.py:79
  479.5 3.9 slice-start
  479.5 4.0 slice-start.1
  486.1 10.4 %copy-start = (bf16[48,384,384]{2,1,0:T(8,128)(2,1)S(1)}, bf16[48,384,384]{2,1,0:T(8,128)(2,1)}, u32[]{:S(2)}) copy-start(bf16[48,384,384]{2,1,0:T(8,128)(2,1)} %all-gather.2.cloned.1.call-done) | copy-start | bytes 42467332
  516.7 79.7 %copy-start.5 = (f32[384,72]{0,1:T(8,128)S(1)}, f32[384,72]{0,1:T(8,128)}, u32[]{:S(2)}) copy-start(f32[384,72]{0,1:T(8,128)} %param.11) | copy-start | bytes 331780
  516.7 79.7 %copy-start.6 = (f32[384,72]{0,1:T(8,128)S(1)}, f32[384,72]{0,1:T(8,128)}, u32[]{:S(2)}) copy-start(f32[384,72]{0,1:T(8,128)} %param.10) | copy-start | bytes 331780
  860.6 18.8 %copy-start.2 = (bf16[768,1,384]{2,0,1:T(8,128)(2,1)S(1)}, bf16[768,1,384]{2,0,1:T(8,128)(2,1)}, u32[]{:S(2)}) copy-start(bf16[768,1,384]{2,0,1:T(8,128)(2,1)} %copy-done.1) | copy-start | bytes 1769476
  860.6 18.8 %copy-start.4 = (bf16[768,1,384]{2,0,1:T(8,128)(2,1)S(1)}, bf16[768,1,384]{2,0,1:T(8,128)(2,1)}, u32[]{:S(2)}) copy-start(bf16[768,1,384]{2,0,1:T(8,128)(2,1)} %copy-done.3) | copy-start | bytes 1769476
Sparse Core Ops, SparseCore 0:
  8.9 93.7 all-gather.1
  526.5 69.8 all-reduce.3
where the time goes:
time: 899 us; the launch traced here: 897 us
  waiting for transfers between devices  444 us (49%)
  blocking collectives  223 us (25%)
  local copies, waits for them, and re-layouts  110 us (12%)
  matrix products  75.2 us (8%)
  other arithmetic  20.4 us (2%)
  between operations  14.2 us (2%)
  starting transfers between devices  10.3 us (1%)
    all_to_all x1, blocking collectives, local(): lax.all_to_all(spectral_sensitivity, 'mp', split_axis=1, concat_axis=0, t...  210 us
    all_to_all x1, waiting for transfers between devices, local(): lax.all_to_all(spec_pred, 'mp', split_axis=0, concat_axis=1, tiled=True)  195 us
    all_to_all x1, waiting for transfers between devices, local(): lax.all_to_all(spec_true, 'mp', split_axis=0, concat_axis=1, tiled=True)  178 us
    psum x1, waiting for transfers between devices, local(): pred_power, true_power = lax.psum((part_pred, part_true), 'mp')  70 us
    reshape x2, local copies, waits for them, and re-layouts, local(): grad_lat = grad_lat.reshape(degrees, lat_dev, 2, channels)  34.8 us
  transfers between devices with their start and end apart: 4, of which 3 were waited for; matrix products, arithmetic and copies ran while one was open for 9% of the time, Pallas kernels for 0%

commit v1 on v0

v1 whole, which is shorter than its diff:
```python
import math

import jax
import jax.numpy as jnp
from jax import lax
from jax.sharding import PartitionSpec as P

MERIDIAN_POINTS = 768
GROUPS = 3


def transform_table(orders, blocks):
    longitude = jnp.arange(MERIDIAN_POINTS, dtype=jnp.int32)
    phase_index = longitude[:, None] * orders[None, :] % MERIDIAN_POINTS
    radians = phase_index.astype(jnp.float32) * (2.0 * math.pi / MERIDIAN_POINTS)
    norm_factor = 1.0 / math.sqrt(MERIDIAN_POINTS)
    cosine = (jnp.cos(radians) * norm_factor).astype(jnp.bfloat16)
    sine = (-jnp.sin(radians) * norm_factor).astype(jnp.bfloat16)
    slots = orders.shape[0] // blocks
    both = jnp.stack(
        [
            cosine.reshape(MERIDIAN_POINTS, blocks, slots),
            sine.reshape(MERIDIAN_POINTS, blocks, slots),
        ],
        axis=2,
    )
    return both.reshape(MERIDIAN_POINTS, 2 * orders.shape[0])


def local(
    blocks,
    prediction_maps,
    observed_maps,
    zonal_wavenumber_map,
    associated_function_table,
    magnitude_factor,
    phase_match_factor,
):
    orders = lax.all_gather(zonal_wavenumber_map, "mp", axis=0, tiled=True)
    fourier = transform_table(orders, blocks)
    full_table = lax.all_gather(associated_function_table, "dp", axis=1, tiled=True)
    channels, lat_dev = prediction_maps.shape[1:3]
    slots, latitudes, degrees = full_table.shape
    part = channels // GROUPS
    order_weight = jnp.where(zonal_wavenumber_map == 0, 1.0, 2.0).astype(jnp.float32)
    magnitude, phase = magnitude_factor.T, phase_match_factor.T

    def to_slots(fields):
        grid = fields.reshape(part * lat_dev, MERIDIAN_POINTS)
        spec = lax.dot_general(
            fourier, grid, (((0,), (1,)), ((), ())), preferred_element_type=jnp.float32
        ).astype(jnp.bfloat16)
        spec = spec.reshape(blocks, 2 * slots, part * lat_dev)
        spec = lax.all_to_all(spec, "mp", split_axis=0, concat_axis=0, tiled=True)
        spec = spec.reshape(blocks, 2, slots, part, lat_dev)
        return spec.transpose(2, 1, 3, 0, 4).reshape(slots, 2 * part, latitudes)

    def analyse(spec):
        return jnp.einsum(
            "sjq,sql->sjl", spec, full_table, preferred_element_type=jnp.float32
        ).reshape(slots, 2, part, degrees)

    def order_power(coef):
        return jnp.sum(order_weight[:, None, None, None] * coef * coef, axis=(0, 1))

    results = []
    for group in range(GROUPS):
        rows = slice(group * part, (group + 1) * part)
        coef_pred = analyse(to_slots(prediction_maps[0, rows]))
        coef_true = analyse(to_slots(observed_maps[0, rows]))
        partial = jnp.stack([order_power(coef_pred), order_power(coef_true)])
        if group > 0:
            partial, _ = lax.optimization_barrier((partial, power))
        power = lax.psum(partial, "mp") + 1.0
        ratio = jnp.sqrt(power[1] / power[0])
        pred_factor = 2.0 * magnitude[rows] * (1.0 - ratio) + 2.0 * phase[rows] * ratio
        true_factor = -2.0 * phase[rows]
        grad_coef = (
            order_weight[:, None, None, None] * (pred_factor * coef_pred + true_factor * coef_true)
        ).astype(jnp.bfloat16)
        grad_spec = jnp.einsum(
            "sjl,sql->sjq",
            grad_coef.reshape(slots, 2 * part, degrees),
            full_table,
            preferred_element_type=jnp.float32,
        ).astype(jnp.bfloat16)
        grad_spec = grad_spec.reshape(slots, 2, part, blocks, lat_dev).transpose(3, 1, 0, 2, 4)
        grad_spec = grad_spec.reshape(blocks, 2 * slots, part * lat_dev)
        grad_lat = lax.all_to_all(grad_spec, "mp", split_axis=0, concat_axis=0, tiled=True)
        grad_grid = lax.dot_general(
            grad_lat.reshape(2 * blocks * slots, part * lat_dev),
            fourier,
            (((0,), (1,)), ((), ())),
            preferred_element_type=jnp.float32,
        ).astype(jnp.bfloat16)
        results.append(grad_grid.reshape(part, lat_dev, MERIDIAN_POINTS))
    return jnp.concatenate(results, axis=0)[None]


def solution(mesh):
    blocks = mesh.shape["mp"]

    def run(*arrays):
        return local(blocks, *arrays)

    return jax.shard_map(
        run,
        mesh=mesh,
        in_specs=(
            P("dp", None, "mp", None),
            P("dp", None, "mp", None),
            P("mp"),
            P("mp", "dp", None),
            P(),
            P(),
        ),
        out_specs=P("dp", None, "mp", None),
        check_vma=False,
    )
```

time: 899 us -> 853 us (0.949); the launches traced: 897 us -> 841 us
  blocking collectives: 223 us -> 13.1 us
  local copies, waits for them, and re-layouts: 110 us -> 220 us
  starting transfers between devices: 10.3 us -> 36.6 us
  matrix products: 75.2 us -> 97.2 us
  waiting for transfers between devices: 444 us -> 432 us
    all_to_all x1 -> x0, blocking collectives: 210 us -> none  [local(): lax.all_to_all(spectral_sensitivity, 'mp', split_axis=1, concat_axis=0, t...]
    reshape x2 -> x27, local copies, waits for them, and re-layouts: 34.8 us -> 201 us  [the longest x12 101 us: to_slots(): spec = spec.reshape(blocks, 2, slots, part, lat_dev)]
    all_to_all x2 -> x9, waiting for transfers between devices: 373 us -> 230 us  [the longest x6 178 us: to_slots(): spec = lax.all_to_all(spec, 'mp', split_axis=0, concat_axis=0, tiled=True)]
    psum x1 -> x3, waiting for transfers between devices: 70 us -> 202 us  [local(): power = lax.psum(partial, 'mp') + 1.0]
    convert_element_type x4 -> x0, local copies, waits for them, and re-layouts: 32.3 us -> none  [the longest x2 16.2 us: local(): spec_true.reshape(degrees, lat_dev, coeff_width).astype(jnp.bfloat16)]
    all_to_all x2 -> x9, starting transfers between devices: 10.1 us -> 36.2 us  [the longest x6 23.4 us: to_slots(): spec = lax.all_to_all(spec, 'mp', split_axis=0, concat_axis=0, tiled=True)]
    dot_general x9 -> x18, matrix products: 75.2 us -> 97.2 us  [the longest x6 31.2 us: analyse(): jnp.einsum('sjq,sql->sjl', spec, full_table, preferred_element_type=jnp.f...]
    concatenate x1 -> x0, local copies, waits for them, and re-layouts: 13.2 us -> none  [local(): spectral_sensitivity = jnp.concatenate([low_part, high_part], axis=0)]
  transfers between devices with their start and end apart: 4 -> 13, of which waited for: 3 -> 11; matrix products, arithmetic and copies ran while one was open for 9% -> 31% of each run, Pallas kernels for 0% -> 0%
where the time goes in v1:
time: 853 us; the launch traced here: 841 us
  waiting for transfers between devices  432 us (51%)
  local copies, waits for them, and re-layouts  220 us (26%)
  matrix products  97.2 us (11%)
  starting transfers between devices  36.6 us (4%)
  other arithmetic  27.2 us (3%)
  between operations  14.6 us (2%)
  blocking collectives  13.1 us (2%)
    psum x3, waiting for transfers between devices, local(): power = lax.psum(partial, 'mp') + 1.0  202 us
    all_to_all x6, waiting for transfers between devices, to_slots(): spec = lax.all_to_all(spec, 'mp', split_axis=0, concat_axis=0, tiled=True)  178 us
    reshape x12, local copies, waits for them, and re-layouts, to_slots(): spec = spec.reshape(blocks, 2, slots, part, lat_dev)  101 us
    all_to_all x3, waiting for transfers between devices, local(): lax.all_to_all(grad_spec, 'mp', split_axis=0, concat_axis=0, tiled=True)  51.2 us
    reshape x6, local copies, waits for them, and re-layouts, to_slots(): return spec.transpose(2, 1, 3, 0, 4).reshape(slots, 2 * part, latitudes)  41.4 us
    reshape x6, local copies, waits for them, and re-layouts, local(): grad_spec.reshape(slots, 2, part, blocks, lat_dev).transpose(3, 1, 0, 2, 4)  37.9 us
    dot_general x6, matrix products, analyse(): jnp.einsum('sjq,sql->sjl', spec, full_table, preferred_element_type=jnp.f...  31.2 us
    dot_general x3, matrix products, local(): jnp.einsum('sjl,sql->sjq', grad_coef.reshape(slots, 2 * part, degrees), f...  30.9 us
  transfers between devices with their start and end apart: 13, of which 11 were waited for; matrix products, arithmetic and copies ran while one was open for 31% of the time, Pallas kernels for 0%

profile of v1, /device:TPU:0, one launch (start us, length us, event | category | flops | bytes accessed | tf_op | source)
XLA Modules:
  0.0 840.8 jit_solution(18001524439011899725)
XLA Ops:
  8.8 13.1 %all-reduce = s32[384]{0:T(512)S(1)} all-reduce(s32[384]{0:T(512)S(1)} %dynamic-update-slice), channel_id=1, replica_groups=mesh['dp'=4,'mp'=8] {'mp'}, use_global_device_ids=true, to_apply=%add | all-reduce | flops 384 | bytes 3072
  21.9 5.4 multiply_convert_fusion.13
  27.5 4.8 fusion.39
  35.2 3.7 all-to-all-start
  38.9 4.2 convolution_convert_fusion.5
  43.1 35.7 %all-to-all-done = bf16[8,96,1152]{2,1,0:T(8,128)(2,1)S(1)} async-done(((bf16[8,96,1152]{2,1,0:T(8,128)(2,1)}), bf16[8,96,1152]{2,1,0:T(8,128)(2,1)S(1)}, u32[]{:S(2)}, u32[]{:S(2)}) %all-to-all-start) | async-done | bytes 1769504 | tf_op jit(solution)/shard_map/all_to_all | solution.py:54
  80.0 3.6 all-to-all-start.3
  83.6 4.8 convolution_convert_fusion.2
  88.4 36.4 %all-to-all-done.3 = bf16[8,96,1152]{2,1,0:T(8,128)(2,1)S(1)} async-done(((bf16[8,96,1152]{2,1,0:T(8,128)(2,1)}), bf16[8,96,1152]{2,1,0:T(8,128)(2,1)S(1)}, u32[]{:S(2)}, u32[]{:S(2)}) %all-to-all-start.3) | async-done | bytes 1769504 | tf_op jit(solution)/shard_map/all_to_all | solution.py:54
  124.8 3.6 all-to-all-start.6
  128.4 4.8 fusion.38
  136.2 33.6 %all-to-all-done.6 = bf16[8,96,1152]{2,1,0:T(8,128)(2,1)S(1)} async-done(((bf16[8,96,1152]{2,1,0:T(8,128)(2,1)}), bf16[8,96,1152]{2,1,0:T(8,128)(2,1)S(1)}, u32[]{:S(2)}, u32[]{:S(2)}) %all-to-all-start.6) | async-done | bytes 1769504 | tf_op jit(solution)/shard_map/all_to_all | solution.py:54
  171.0 3.6 all-to-all-start.4
  174.7 4.8 convolution_convert_fusion.1
  179.5 36.6 %all-to-all-done.4 = bf16[8,96,1152]{2,1,0:T(8,128)(2,1)S(1)} async-done(((bf16[8,96,1152]{2,1,0:T(8,128)(2,1)}), bf16[8,96,1152]{2,1,0:T(8,128)(2,1)S(1)}, u32[]{:S(2)}, u32[]{:S(2)}) %all-to-all-start.4) | async-done | bytes 1769504 | tf_op jit(solution)/shard_map/all_to_all | solution.py:54
  217.4 4.3 all-to-all-start.7
  221.7 4.8 convolution_convert_fusion.7
  226.5 36.0 %all-to-all-done.7 = bf16[8,96,1152]{2,1,0:T(8,128)(2,1)} async-done(((bf16[8,96,1152]{2,1,0:T(8,128)(2,1)}), bf16[8,96,1152]{2,1,0:T(8,128)(2,1)}, u32[]{:S(2)}, u32[]{:S(2)}) %all-to-all-start.7) | async-done | bytes 1769504 | tf_op jit(solution)/shard_map/all_to_all | solution.py:54
  262.5 4.4 all-to-all-start.1
  267.3 5.6 reshape.220
  272.9 9.9 %copy.42 = bf16[8,2,48,24,48]{4,0,3,1,2:T(8,128)(2,1)} copy(bf16[8,2,48,24,48]{4,3,2,1,0:T(8,128)(2,1)} %reshape.220) | data formatting | bytes 3538944 | tf_op jit(solution)/shard_map/reshape | solution.py:55
  282.8 6.3 reshape.221
  289.1 6.1 reshape.210
  295.2 9.9 %copy.45 = bf16[8,2,48,24,48]{4,0,3,1,2:T(8,128)(2,1)} copy(bf16[8,2,48,24,48]{4,3,2,1,0:T(8,128)(2,1)} %reshape.210) | data formatting | bytes 3538944 | tf_op jit(solution)/shard_map/reshape | solution.py:55
  305.1 6.3 reshape.211
  311.4 7.4 reshape.200
  318.8 9.9 %copy.48 = bf16[8,2,48,24,48]{4,0,3,1,2:T(8,128)(2,1)} copy(bf16[8,2,48,24,48]{4,3,2,1,0:T(8,128)(2,1)} %reshape.200) | data formatting | bytes 3538944 | tf_op jit(solution)/shard_map/reshape | solution.py:55
  328.7 7.2 reshape.201
  335.9 7.4 reshape.223
  343.3 9.9 %copy.41 = bf16[8,2,48,24,48]{4,0,3,1,2:T(8,128)(2,1)} copy(bf16[8,2,48,24,48]{4,3,2,1,0:T(8,128)(2,1)} %reshape.223) | data formatting | bytes 3538944 | tf_op jit(solution)/shard_map/reshape | solution.py:55
  353.2 7.2 reshape.224
  360.4 7.4 reshape.213
  367.8 9.9 %copy.44 = bf16[8,2,48,24,48]{4,0,3,1,2:T(8,128)(2,1)} copy(bf16[8,2,48,24,48]{4,3,2,1,0:T(8,128)(2,1)} %reshape.213) | data formatting | bytes 3538944 | tf_op jit(solution)/shard_map/reshape | solution.py:55
  377.7 7.2 reshape.214
  384.9 7.7 reshape.203
  392.5 9.9 %copy.47 = bf16[8,2,48,24,48]{4,0,3,1,2:T(8,128)(2,1)} copy(bf16[8,2,48,24,48]{4,3,2,1,0:T(8,128)(2,1)} %reshape.203) | data formatting | bytes 3538944 | tf_op jit(solution)/shard_map/reshape | solution.py:55
  402.4 7.3 reshape.204
  409.8 9.2 %fusion.43 = f32[48,48,384]{2,1,0:T(8,128)} fusion(bf16[48,48,384]{2,1,0:T(8,128)(2,1)S(1)} %reshape.221, bf16[48,384,384]{2,1,0:T(8,128)(2,1)} %all-gather.2.cloned.1.call-done), kind=kOutput, calls=%fused_computation.92 | convolution fusion | flops 679477248 | bytes 19464192 | tf_op jit(solution)/shard_map/sjq,sql->sjl/dot_general | solution.py:59
  422.4 4.0 fusion.44
  431.4 11.5 %fusion = (f32[48,384]{1,0:T(8,128)}, f32[48,384]{1,0:T(8,128)}, f32[48,384]{1,0:T(8,128)}, f32[48,384]{1,0:T(8,128)}, f32[48,384]{1,0:T(8,128)}, /*index=5*/f32[48,384]{1,0:T(8,128)}, f32[48,48,384]{2,1,0:T(8,128)}) fusion(f32[48]{0:T(128)S(1)} %compare_select_fusion, f32[48,48,384]{2,1,0:T(8,128)S(1)} %fusion.40, f32[48,48,384]{2,1,0:T(8,128)S(1)} %fusion.41, ...), kind=kOutput, calls=%fused_computation.16 | convolution fusion | flops 695291904 | bytes 37601472 | tf_op jit(solution)/shard_map/sjq,sql->sjl/dot_general | solution.py:59
  454.8 62.4 %all-reduce.5.cloned.1.call-done = f32[2,24,384]{2,1,0:T(8,128)} async-done(((f32[2,24,384]{2,1,0:T(8,128)}), f32[2,24,384]{2,1,0:T(8,128)}) %all-reduce.5.cloned.1.call-update) | async-done | bytes 73744 | tf_op jit(solution)/shard_map/psum | solution.py:74
  520.2 68.9 %all-reduce.7.cloned.1.call-done = f32[2,24,384]{2,1,0:T(8,128)} async-done(((f32[2,24,384]{2,1,0:T(8,128)}), f32[2,24,384]{2,1,0:T(8,128)}) %all-reduce.7.cloned.1.call-update) | async-done | bytes 73744 | tf_op jit(solution)/shard_map/psum | solution.py:74
  590.7 70.2 %all-reduce.9.cloned.1.call-done = f32[2,24,384]{2,1,0:T(8,128)} async-done(((f32[2,24,384]{2,1,0:T(8,128)}), f32[2,24,384]{2,1,0:T(8,128)}) %all-reduce.9.cloned.1.call-update) | async-done | bytes 73744 | tf_op jit(solution)/shard_map/psum | solution.py:74
  663.4 10.6 %fusion.18 = bf16[48,48,384]{2,1,0:T(8,128)(2,1)} fusion(bf16[48,384,384]{2,1,0:T(8,128)(2,1)} %all-gather.2.cloned.1.call-done, f32[48,48,384]{2,1,0:T(8,128)} %fusion.44, f32[48,48,384]{2,1,0:T(8,128)} %fusion.43, f32[48,384]{1,0:T(8,128)S(1)} %bitcast.169, f32[48,384]{1,0:T(8,128)S(1)} %bitcast.167, f32[48]{0:T(128)S(1)} %compare_select_fusion), kind=kOutput, calls=%fused_computation.47 | convolution fusion | flops 684785664 | bytes 23150784 | tf_op jit(solution)/shard_map/sjl,sql->sjq/dot_general | solution.py:81
  674.0 7.3 reshape.225
  681.3 5.4 copy.40
  686.7 7.0 reshape.226
  693.6 4.6 all-to-all-start.8
  699.8 10.6 %fusion.19 = bf16[48,48,384]{2,1,0:T(8,128)(2,1)} fusion(bf16[48,384,384]{2,1,0:T(8,128)(2,1)} %all-gather.2.cloned.1.call-done, f32[48,48,384]{2,1,0:T(8,128)} %copy-done.2, f32[48,48,384]{2,1,0:T(8,128)} %copy-done.1, f32[48,384]{1,0:T(8,128)S(1)} %bitcast.170, f32[48,384]{1,0:T(8,128)S(1)} %bitcast.168, f32[48]{0:T(128)S(1)} %compare_select_fusion), kind=kOutput, calls=%fused_computation.48 | convolution fusion | flops 684785664 | bytes 23150784 | tf_op jit(solution)/shard_map/sjl,sql->sjq/dot_general | solution.py:81
  710.4 7.3 reshape.215
  717.7 5.4 copy.43
  723.0 7.0 reshape.216
  730.0 7.8 all-to-all-done.8
  737.8 4.6 all-to-all-start.5
  743.9 9.6 %fusion.20 = bf16[48,48,384]{2,1,0:T(8,128)(2,1)} fusion(bf16[48,384,384]{2,1,0:T(8,128)(2,1)} %all-gather.2.cloned.1.call-done, f32[48,48,384]{2,1,0:T(8,128)S(1)} %fusion.40, f32[48,48,384]{2,1,0:T(8,128)} %get-tuple-element.29, f32[48,384]{1,0:T(8,128)S(1)} %bitcast.166, f32[48,384]{1,0:T(8,128)S(1)} %bitcast.165, f32[48]{0:T(128)S(1)} %compare_select_fusion), kind=kOutput, calls=%fused_computation.49 | convolution fusion | flops 684785664 | bytes 23150784 | tf_op jit(solution)/shard_map/sjl,sql->sjq/dot_general | solution.py:81
  753.6 7.3 reshape.205
  760.9 5.4 copy.46
  766.2 7.0 reshape.206
  773.2 9.8 %all-to-all-done.5 = bf16[8,96,1152]{2,1,0:T(8,128)(2,1)} async-done(((bf16[8,96,1152]{2,1,0:T(8,128)(2,1)}), bf16[8,96,1152]{2,1,0:T(8,128)(2,1)}, u32[]{:S(2)}, u32[]{:S(2)}) %all-to-all-start.5) | async-done | bytes 1769504 | tf_op jit(solution)/shard_map/all_to_all | solution.py:89
  783.0 3.6 all-to-all-start.2
  786.6 3.5 convolution_convert_fusion
  790.1 4.3 convolution_convert_fusion.3
  794.4 33.6 %all-to-all-done.2 = bf16[8,96,1152]{2,1,0:T(8,128)(2,1)S(1)} async-done(((bf16[8,96,1152]{2,1,0:T(8,128)(2,1)}), bf16[8,96,1152]{2,1,0:T(8,128)(2,1)S(1)}, u32[]{:S(2)}, u32[]{:S(2)}) %all-to-all-start.2) | async-done | bytes 1769504 | tf_op jit(solution)/shard_map/all_to_all | solution.py:89
  828.0 3.0 convolution_convert_fusion.6
  (75 shorter events, 44.9 us)
Async XLA Ops:
  6.5 0.7 copy-start.16
  6.5 2.0 copy-start.15
  6.5 403.3 %all-gather.2.cloned.1.call-start = ((), (), s32[]{:S(2)}) async-start(), calls=%async_computation.9 | async-start | bytes 17694720 | tf_op jit(solution)/shard_map/all_gather | solution.py:41
  27.5 4.8 copy-start.12
  35.2 43.6 %all-to-all-start = ((bf16[8,96,1152]{2,1,0:T(8,128)(2,1)}), bf16[8,96,1152]{2,1,0:T(8,128)(2,1)S(1)}, u32[]{:S(2)}, u32[]{:S(2)}) async-start(bf16[8,96,1152]{2,1,0:T(8,128)(2,1)} %bitcast.4), calls=%async_computation | async-start | bytes 3538944 | tf_op jit(solution)/shard_map/all_to_all | solution.py:54
  78.8 1.2 copy-start.6
  80.0 44.8 %all-to-all-start.3 = ((bf16[8,96,1152]{2,1,0:T(8,128)(2,1)}), bf16[8,96,1152]{2,1,0:T(8,128)(2,1)S(1)}, u32[]{:S(2)}, u32[]{:S(2)}) async-start(bf16[8,96,1152]{2,1,0:T(8,128)(2,1)} %bitcast.144), calls=%async_computation.3 | async-start | bytes 3538944 | tf_op jit(solution)/shard_map/all_to_all | solution.py:54
  124.8 45.0 %all-to-all-start.6 = ((bf16[8,96,1152]{2,1,0:T(8,128)(2,1)}), bf16[8,96,1152]{2,1,0:T(8,128)(2,1)S(1)}, u32[]{:S(2)}, u32[]{:S(2)}) async-start(bf16[8,96,1152]{2,1,0:T(8,128)(2,1)} %bitcast.142), calls=%async_computation.6 | async-start | bytes 3538944 | tf_op jit(solution)/shard_map/all_to_all | solution.py:54
  128.4 4.8 copy-start.13
  169.8 1.2 copy-start.8
  171.0 45.0 %all-to-all-start.4 = ((bf16[8,96,1152]{2,1,0:T(8,128)(2,1)}), bf16[8,96,1152]{2,1,0:T(8,128)(2,1)S(1)}, u32[]{:S(2)}, u32[]{:S(2)}) async-start(bf16[8,96,1152]{2,1,0:T(8,128)(2,1)} %bitcast.146), calls=%async_computation.4 | async-start | bytes 3538944 | tf_op jit(solution)/shard_map/all_to_all | solution.py:54
  216.1 1.3 copy-start.7
  217.4 45.2 %all-to-all-start.7 = ((bf16[8,96,1152]{2,1,0:T(8,128)(2,1)}), bf16[8,96,1152]{2,1,0:T(8,128)(2,1)}, u32[]{:S(2)}, u32[]{:S(2)}) async-start(bf16[8,96,1152]{2,1,0:T(8,128)(2,1)} %bitcast.145), calls=%async_computation.7 | async-start | bytes 3538944 | tf_op jit(solution)/shard_map/all_to_all | solution.py:54
  262.5 4.8 copy-start.9
  262.5 122.4 %all-to-all-start.1 = ((bf16[8,96,1152]{2,1,0:T(8,128)(2,1)}), bf16[8,96,1152]{2,1,0:T(8,128)(2,1)}, u32[]{:S(2)}, u32[]{:S(2)}) async-start(bf16[8,96,1152]{2,1,0:T(8,128)(2,1)} %bitcast.141), calls=%async_computation.1 | async-start | bytes 3538944 | tf_op jit(solution)/shard_map/all_to_all | solution.py:54
  267.0 250.2 %all-reduce.5.cloned.1.call-start = ((), (), s32[]{:S(2)}) async-start(), calls=%async_computation.10 | async-start | bytes 147456 | tf_op jit(solution)/shard_map/psum | solution.py:74
  409.8 10.3 %copy-start = (bf16[48,384,384]{2,1,0:T(8,128)(2,1)S(1)}, bf16[48,384,384]{2,1,0:T(8,128)(2,1)}, u32[]{:S(2)}) copy-start(bf16[48,384,384]{2,1,0:T(8,128)(2,1)} %all-gather.2.cloned.1.call-done) | copy-start | bytes 42467332
  420.1 2.2 copy-start.3
  422.4 8.4 %copy-start.1 = (f32[48,48,384]{2,1,0:T(8,128)}, f32[48,48,384]{2,1,0:T(8,128)S(1)}, u32[]{:S(2)}) copy-start(f32[48,48,384]{2,1,0:T(8,128)S(1)} %fusion.41) | copy-start | bytes 10616836
  422.4 4.0 copy-start.4
  426.4 2.2 copy-start.5
  428.6 2.2 copy-start.2
  428.6 2.8 copy-start.10
  447.3 141.8 %all-reduce.7.cloned.1.call-start = ((), (), s32[]{:S(2)}) async-start(), calls=%async_computation.11 | async-start | bytes 147456 | tf_op jit(solution)/shard_map/psum | solution.py:74
  518.7 142.1 %all-reduce.9.cloned.1.call-start = ((), (), s32[]{:S(2)}) async-start(), calls=%async_computation.12 | async-start | bytes 147456 | tf_op jit(solution)/shard_map/psum | solution.py:74
  693.6 44.2 %all-to-all-start.8 = ((bf16[8,96,1152]{2,1,0:T(8,128)(2,1)}), bf16[8,96,1152]{2,1,0:T(8,128)(2,1)}, u32[]{:S(2)}, u32[]{:S(2)}) async-start(bf16[8,96,1152]{2,1,0:T(8,128)(2,1)} %reshape.226), calls=%async_computation.8 | async-start | bytes 3538944 | tf_op jit(solution)/shard_map/all_to_all | solution.py:89
  737.8 45.2 %all-to-all-start.5 = ((bf16[8,96,1152]{2,1,0:T(8,128)(2,1)}), bf16[8,96,1152]{2,1,0:T(8,128)(2,1)}, u32[]{:S(2)}, u32[]{:S(2)}) async-start(bf16[8,96,1152]{2,1,0:T(8,128)(2,1)} %reshape.216), calls=%async_computation.5 | async-start | bytes 3538944 | tf_op jit(solution)/shard_map/all_to_all | solution.py:89
  783.0 45.0 %all-to-all-start.2 = ((bf16[8,96,1152]{2,1,0:T(8,128)(2,1)}), bf16[8,96,1152]{2,1,0:T(8,128)(2,1)S(1)}, u32[]{:S(2)}, u32[]{:S(2)}) async-start(bf16[8,96,1152]{2,1,0:T(8,128)(2,1)} %reshape.206), calls=%async_computation.2 | async-start | bytes 3538944 | tf_op jit(solution)/shard_map/all_to_all | solution.py:89
  786.6 3.5 copy-start.14
  828.0 3.0 copy-start.11
Sparse Core Ops, SparseCore 0:
  8.9 93.7 all-gather.1
  447.4 69.7 all-reduce.4
  520.6 68.4 all-reduce.6
  592.4 68.4 all-reduce.8

commit v2 on v1

v2 whole, which is shorter than its diff:
```python
import math

import jax
import jax.numpy as jnp
from jax import lax
from jax.sharding import PartitionSpec as P

MERIDIAN_POINTS = 768
CUTS = (0, 3, 6, 8, 9)


def transform_table(orders, blocks):
    longitude = jnp.arange(MERIDIAN_POINTS, dtype=jnp.int32)
    phase_index = longitude[:, None] * orders[None, :] % MERIDIAN_POINTS
    radians = phase_index.astype(jnp.float32) * (2.0 * math.pi / MERIDIAN_POINTS)
    norm_factor = 1.0 / math.sqrt(MERIDIAN_POINTS)
    cosine = (jnp.cos(radians) * norm_factor).astype(jnp.bfloat16)
    sine = (-jnp.sin(radians) * norm_factor).astype(jnp.bfloat16)
    slots = orders.shape[0] // blocks
    both = jnp.stack(
        [
            cosine.reshape(MERIDIAN_POINTS, blocks, slots),
            sine.reshape(MERIDIAN_POINTS, blocks, slots),
        ],
        axis=2,
    )
    return both.reshape(MERIDIAN_POINTS, 2 * orders.shape[0])


def local(
    blocks,
    prediction_maps,
    observed_maps,
    zonal_wavenumber_map,
    associated_function_table,
    magnitude_factor,
    phase_match_factor,
):
    last = [zonal_wavenumber_map]

    def exchange(array):
        array, _ = lax.optimization_barrier((array, last[0]))
        last[0] = lax.all_to_all(array, "mp", split_axis=0, concat_axis=0, tiled=True)
        return last[0]

    def share(array):
        return exchange(jnp.broadcast_to(array[None], (blocks,) + array.shape))

    channels, lat_dev = prediction_maps.shape[1:3]
    slots = zonal_wavenumber_map.shape[0]
    full_table = lax.all_gather(associated_function_table, "dp", axis=1, tiled=True)
    latitudes, degrees = full_table.shape[1:]
    orders = share(zonal_wavenumber_map[None]).reshape(blocks * slots)
    fourier = transform_table(orders, blocks)
    order_weight = jnp.where(zonal_wavenumber_map == 0, 1.0, 2.0).astype(jnp.float32)
    magnitude, phase = magnitude_factor.T, phase_match_factor.T

    def to_slots(rows):
        part = rows.stop - rows.start
        grid = jnp.concatenate([prediction_maps[0, rows], observed_maps[0, rows]], axis=0)
        spec = lax.dot_general(
            fourier,
            grid.reshape(2 * part * lat_dev, MERIDIAN_POINTS),
            (((0,), (1,)), ((), ())),
            preferred_element_type=jnp.float32,
        ).astype(jnp.bfloat16)
        return exchange(spec.reshape(blocks, 2 * slots, 2 * part * lat_dev))

    def analyse(spec, rows):
        part = rows.stop - rows.start
        spec = spec.reshape(blocks, 2, slots, 2 * part, lat_dev)
        spec = spec.transpose(2, 1, 3, 0, 4).reshape(slots, 4 * part, latitudes)
        coef = jnp.einsum("sjq,sql->sjl", spec, full_table, preferred_element_type=jnp.float32)
        coef = coef.reshape(slots, 2, 2, part, degrees)
        return coef, jnp.sum(order_weight[:, None, None, None, None] * coef * coef, axis=(0, 1))

    def sum_orders(power):
        width = math.gcd(128, power.size // blocks)
        pieces = exchange(power.reshape(blocks, power.size // (blocks * width), width))
        return share(jnp.sum(pieces, axis=0)).reshape(power.shape) + 1.0

    def synthesise(coef, power, rows):
        part = rows.stop - rows.start
        ratio = jnp.sqrt(power[1] / power[0])
        pred_factor = 2.0 * magnitude[rows] * (1.0 - ratio) + 2.0 * phase[rows] * ratio
        true_factor = -2.0 * phase[rows]
        grad_coef = (
            order_weight[:, None, None, None]
            * (pred_factor * coef[:, :, 0] + true_factor * coef[:, :, 1])
        ).astype(jnp.bfloat16)
        grad_spec = jnp.einsum(
            "sjl,sql->sjq",
            grad_coef.reshape(slots, 2 * part, degrees),
            full_table,
            preferred_element_type=jnp.float32,
        ).astype(jnp.bfloat16)
        grad_spec = grad_spec.reshape(slots, 2, part, blocks, lat_dev).transpose(3, 1, 0, 2, 4)
        return grad_spec.reshape(blocks, 2 * slots, part * lat_dev)

    def to_grid(grad_spec, rows):
        part = rows.stop - rows.start
        grad_grid = lax.dot_general(
            exchange(grad_spec).reshape(2 * blocks * slots, part * lat_dev),
            fourier,
            (((0,), (1,)), ((), ())),
            preferred_element_type=jnp.float32,
        ).astype(jnp.bfloat16)
        return grad_grid.reshape(part, lat_dev, MERIDIAN_POINTS)

    bounds = [channels * cut // 9 for cut in CUTS]
    groups = [slice(low, high) for low, high in zip(bounds[:-1], bounds[1:])]
    count = len(groups)
    spec, coef, power, grad, results = {}, {}, {}, {}, {}

    def forward(group):
        spec[group] = to_slots(groups[group])

    def legendre(group):
        coef[group], partial = analyse(spec[group], groups[group])
        power[group] = sum_orders(partial)
        grad[group] = synthesise(coef[group], power[group], groups[group])

    def backward(group):
        results[group] = to_grid(grad[group], groups[group])

    forward(0)
    for group in range(1, count):
        forward(group)
        legendre(group - 1)
    for group in range(count - 2):
        backward(group)
    legendre(count - 1)
    backward(count - 2)
    backward(count - 1)
    return jnp.concatenate([results[group] for group in range(count)], axis=0)[None]


def solution(mesh):
    blocks = mesh.shape["mp"]

    def run(*arrays):
        return local(blocks, *arrays)

    return jax.shard_map(
        run,
        mesh=mesh,
        in_specs=(
            P("dp", None, "mp", None),
            P("dp", None, "mp", None),
            P("mp"),
            P("mp", "dp", None),
            P(),
            P(),
        ),
        out_specs=P("dp", None, "mp", None),
        check_vma=False,
    )
```

time: 853 us -> 674 us (0.79)
  waiting for transfers between devices: 432 us -> 194 us
  starting transfers between devices: 36.6 us -> 80.9 us
  matrix products: 97.2 us -> 114 us
    psum x3 -> x0, waiting for transfers between devices: 202 us -> none  [local(): power = lax.psum(partial, 'mp') + 1.0]
    all_to_all x9 -> x16, starting transfers between devices: 36.2 us -> 80.9 us  [exchange(): lax.all_to_all(array, 'mp', split_axis=0, concat_axis=0, tiled=True)]
    all_to_all x9 -> x16, waiting for transfers between devices: 230 us -> 193 us  [exchange(): lax.all_to_all(array, 'mp', split_axis=0, concat_axis=0, tiled=True)]
    unnamed x1 -> x0, blocking collectives: 13.1 us -> none
    dot_general x6 -> x4, matrix products: 31.2 us -> 43.2 us  [analyse(): jnp.einsum('sjq,sql->sjl', spec, full_table, preferred_element_type=jnp.f...]
    reshape x27 -> x28, local copies, waits for them, and re-layouts: 201 us -> 190 us  [the longest x8 98.3 us: analyse(): spec = spec.reshape(blocks, 2, slots, 2 * part, lat_dev)]
    all_to_all x0 -> x1, blocking collectives: none -> 10.1 us  [exchange(): lax.all_to_all(array, 'mp', split_axis=0, concat_axis=0, tiled=True)]
    slice x2 -> x3, local copies, waits for them, and re-layouts: 9.61 us -> 17.1 us  [synthesise(): coef[:, :, 0]]
  transfers between devices with their start and end apart: 13 -> 17, of which waited for: 11 -> 11; matrix products, arithmetic and copies ran while one was open for 31% -> 50% of each run, Pallas kernels for 0% -> 0%
where the time goes in v2:
time: 674 us; the launch traced here: 665 us
  local copies, waits for them, and re-layouts  223 us (33%)
  waiting for transfers between devices  194 us (29%)
  matrix products  114 us (17%)
  starting transfers between devices  80.9 us (12%)
  other arithmetic  29.6 us (4%)
  between operations  14.1 us (2%)
  blocking collectives  10.1 us (1%)
    all_to_all x16, waiting for transfers between devices, exchange(): lax.all_to_all(array, 'mp', split_axis=0, concat_axis=0, tiled=True)  193 us
    reshape x8, local copies, waits for them, and re-layouts, analyse(): spec = spec.reshape(blocks, 2, slots, 2 * part, lat_dev)  98.3 us
    all_to_all x16, starting transfers between devices, exchange(): lax.all_to_all(array, 'mp', split_axis=0, concat_axis=0, tiled=True)  80.9 us
    dot_general x4, matrix products, analyse(): jnp.einsum('sjq,sql->sjl', spec, full_table, preferred_element_type=jnp.f...  43.2 us
    dot_general x4, matrix products, synthesise(): jnp.einsum('sjl,sql->sjq', grad_coef.reshape(slots, 2 * part, degrees), f...  39.8 us
    reshape x4, local copies, waits for them, and re-layouts, analyse(): spec = spec.transpose(2, 1, 3, 0, 4).reshape(slots, 4 * part, latitudes)  39.3 us
    reshape x8, local copies, waits for them, and re-layouts, synthesise(): grad_spec.reshape(slots, 2, part, blocks, lat_dev).transpose(3, 1, 0, 2, 4)  29.7 us
    reshape x4, local copies, waits for them, and re-layouts, synthesise(): return grad_spec.reshape(blocks, 2 * slots, part * lat_dev)  21.2 us
  transfers between devices with their start and end apart: 17, of which 11 were waited for; matrix products, arithmetic and copies ran while one was open for 50% of the time, Pallas kernels for 0%

profile of v2, /device:TPU:0, one launch (start us, length us, event | category | flops | bytes accessed | tf_op | source)
XLA Modules:
  0.0 665.0 jit_solution(7312527743844706504)
XLA Ops:
  7.9 7.3 %all-to-all-start = ((s32[8,1,48]{2,1,0:T(1,128)}), s32[8,1,48]{2,1,0:T(1,128)S(1)}, u32[]{:S(2)}, u32[]{:S(2)}) async-start(s32[8,1,48]{2,1,0:T(1,128)} %broadcast_in_dim.22), calls=%async_computation | async-start | bytes 8192 | tf_op jit(solution)/shard_map/all_to_all | solution.py:43
  21.8 5.4 multiply_convert_fusion.1
  27.4 4.4 convolution_convert_fusion.1
  31.8 6.0 all-to-all-start.1
  37.8 7.1 %convolution_convert_fusion = bf16[768,2304]{1,0:T(8,128)(2,1)} fusion(bf16[768,768]{0,1:T(8,128)(2,1)} %bitcast.202, bf16[2304,768]{1,0:T(8,128)(2,1)} %bitcast.193), kind=kOutput, calls=%fused_computation.9 | convolution fusion | flops 2719678464 | bytes 8257536 | tf_op jit(solution)/shard_map/dot_general | solution.py:61
  44.9 71.0 %all-to-all-done.1 = bf16[8,96,2304]{2,1,0:T(8,128)(2,1)S(1)} async-done(((bf16[8,96,2304]{2,1,0:T(8,128)(2,1)}), bf16[8,96,2304]{2,1,0:T(8,128)(2,1)S(1)}, u32[]{:S(2)}, u32[]{:S(2)}) %all-to-all-start.1) | async-done | bytes 3538976 | tf_op jit(solution)/shard_map/all_to_all | solution.py:43
  115.9 4.5 all-to-all-start.2
  120.4 3.2 slice_bitcast_fusion.6
  123.7 14.1 %reshape.277 = bf16[8,2,48,48,48]{4,3,2,1,0:T(8,128)(2,1)} reshape(bf16[8,96,2304]{2,1,0:T(8,128)(2,1)S(1)} %all-to-all-done.1) | data formatting | bytes 7077888 | tf_op jit(solution)/shard_map/reshape | solution.py:71
  137.8 18.2 %copy.44 = bf16[8,2,48,48,48]{4,0,3,1,2:T(8,128)(2,1)} copy(bf16[8,2,48,48,48]{4,3,2,1,0:T(8,128)(2,1)} %reshape.277) | data formatting | bytes 7077888 | tf_op jit(solution)/shard_map/reshape | solution.py:71
  156.0 12.9 %reshape.278 = bf16[48,96,384]{2,1,0:T(8,128)(2,1)} reshape(bf16[48,2,48,8,48]{4,3,2,1,0:T(8,128)(2,1)} %bitcast.183) | data formatting | bytes 7077888 | tf_op jit(solution)/shard_map/reshape | solution.py:72
  168.9 30.0 %all-to-all-done.2 = bf16[8,96,2304]{2,1,0:T(8,128)(2,1)} async-done(((bf16[8,96,2304]{2,1,0:T(8,128)(2,1)}), bf16[8,96,2304]{2,1,0:T(8,128)(2,1)}, u32[]{:S(2)}, u32[]{:S(2)}) %all-to-all-start.2) | async-done | bytes 3538976 | tf_op jit(solution)/shard_map/all_to_all | solution.py:43
  199.0 15.7 %reshape.292 = bf16[8,2,48,48,48]{4,3,2,1,0:T(8,128)(2,1)} reshape(bf16[8,96,2304]{2,1,0:T(8,128)(2,1)} %all-to-all-done.2) | data formatting | bytes 7077888 | tf_op jit(solution)/shard_map/reshape | solution.py:71
  214.7 18.1 %copy.43 = bf16[8,2,48,48,48]{4,0,3,1,2:T(8,128)(2,1)} copy(bf16[8,2,48,48,48]{4,3,2,1,0:T(8,128)(2,1)} %reshape.292) | data formatting | bytes 7077888 | tf_op jit(solution)/shard_map/reshape | solution.py:71
  232.9 13.1 %reshape.293 = bf16[48,96,384]{2,1,0:T(8,128)(2,1)} reshape(bf16[48,2,48,8,48]{4,3,2,1,0:T(8,128)(2,1)} %bitcast.184) | data formatting | bytes 7077888 | tf_op jit(solution)/shard_map/reshape | solution.py:72
  246.0 11.9 %fusion.42 = f32[48,96,384]{2,1,0:T(8,128)} fusion(bf16[48,96,384]{2,1,0:T(8,128)(2,1)} %reshape.293, bf16[48,384,384]{2,1,0:T(8,128)(2,1)} %all-gather.2.cloned.1.call-done), kind=kOutput, calls=%fused_computation.110 | convolution fusion | flops 1358954496 | bytes 24772608 | tf_op jit(solution)/shard_map/sjq,sql->sjl/dot_general | solution.py:73
  257.8 10.7 %fusion = (f32[96,384]{1,0:T(8,128)S(1)}, f32[96,384]{1,0:T(8,128)S(1)}, f32[48,96,384]{2,1,0:T(8,128)}) fusion(f32[48]{0:T(128)S(1)} %compare_select_fusion, f32[48,96,384]{2,1,0:T(8,128)} %fusion.42, bf16[48,96,384]{2,1,0:T(8,128)(2,1)} %reshape.278, bf16[48,384,384]{2,1,0:T(8,128)(2,1)S(1)} %copy-done), kind=kOutput, calls=%fused_computation.4 | convolution fusion | flops 1369497600 | bytes 32145600 | tf_op jit(solution)/shard_map/sjq,sql->sjl/dot_general | solution.py:73
  269.2 3.6 all-to-all-start.3
  275.8 4.1 all-to-all-done.3
  280.6 3.4 all-to-all-start.4
  284.0 5.2 convolution_convert_fusion.2
  291.7 4.0 all-to-all-start.5
  300.2 47.9 %all-to-all-done.5 = bf16[8,96,1536]{2,1,0:T(8,128)(2,1)S(1)} async-done(((bf16[8,96,1536]{2,1,0:T(8,128)(2,1)}), bf16[8,96,1536]{2,1,0:T(8,128)(2,1)S(1)}, u32[]{:S(2)}, u32[]{:S(2)}) %all-to-all-start.5) | async-done | bytes 2359328 | tf_op jit(solution)/shard_map/all_to_all | solution.py:43
  348.1 3.6 all-to-all-start.6
  351.7 6.4 fusion.39
  359.5 5.3 all-to-all-start.7
  364.8 6.4 fusion.40
  372.5 5.6 all-to-all-start.8
  381.1 7.6 %reshape.287 = bf16[8,2,48,32,48]{4,3,2,1,0:T(8,128)(2,1)} reshape(bf16[8,96,1536]{2,1,0:T(8,128)(2,1)S(1)} %all-to-all-done.5) | data formatting | bytes 4718592 | tf_op jit(solution)/shard_map/reshape | solution.py:71
  388.6 12.7 %copy.45 = bf16[8,2,48,32,48]{4,0,3,1,2:T(8,128)(2,1)} copy(bf16[8,2,48,32,48]{4,3,2,1,0:T(8,128)(2,1)} %reshape.287) | data formatting | bytes 4718592 | tf_op jit(solution)/shard_map/reshape | solution.py:71
  401.4 8.1 %reshape.288 = bf16[48,64,384]{2,1,0:T(8,128)(2,1)S(1)} reshape(bf16[48,2,32,8,48]{4,3,2,1,0:T(8,128)(2,1)} %bitcast.186) | data formatting | bytes 4718592 | tf_op jit(solution)/shard_map/reshape | solution.py:72
  409.4 10.4 %fusion.2 = (f32[64,384]{1,0:T(8,128)}, f32[48,64,384]{2,1,0:T(8,128)}) fusion(f32[48]{0:T(128)S(1)} %compare_select_fusion, bf16[48,64,384]{2,1,0:T(8,128)(2,1)S(1)} %reshape.288, bf16[48,384,384]{2,1,0:T(8,128)(2,1)} %all-gather.2.cloned.1.call-done), kind=kOutput, calls=%fused_computation.11 | convolution fusion | flops 909484032 | bytes 21332160 | tf_op jit(solution)/shard_map/sjq,sql->sjl/dot_general | solution.py:73
  423.1 6.4 all-to-all-start.9
  429.7 7.5 %fusion.8 = (bf16[48,48,384]{2,1,0:T(8,128)(2,1)}, bf16[48,48,384]{2,1,0:T(8,128)(2,1)S(1)}) fusion(f32[48,2,1,24,384]{4,3,2,1,0:T(8,128)} %get-tuple-element.42, f32[48,2,1,24,384]{4,3,2,1,0:T(8,128)} %get-tuple-element.41, f32[48,384]{1,0:T(8,128)S(1)} %bitcast.219, f32[48,384]{1,0:T(8,128)S(1)} %bitcast.218, f32[48]{0:T(128)S(1)} %compare_select_fusion, ...), kind=kLoop, calls=%fused_computation.24 | loop fusion | flops 8847360 | bytes 17989824 | tf_op jit(solution)/shard_map/convert_element_type | solution.py:90
  437.9 6.0 all-to-all-start.10
  443.9 10.3 %convolution_convert_fusion.6 = bf16[48,48,384]{2,1,0:T(8,128)(2,1)S(1)} fusion(bf16[48,48,384]{2,1,0:T(8,128)(2,1)} %get-tuple-element.63, bf16[48,384,384]{2,1,0:T(8,128)(2,1)} %all-gather.2.cloned.1.call-done), kind=kOutput, calls=%fused_computation.45 | convolution fusion | flops 680361984 | bytes 17694720 | tf_op jit(solution)/shard_map/sjl,sql->sjq/dot_general | solution.py:91
  454.2 5.4 reshape.283
  459.6 5.4 copy.47
  464.9 6.9 %reshape.284 = bf16[8,96,1152]{2,1,0:T(8,128)(2,1)} reshape(bf16[8,2,48,24,48]{4,3,2,1,0:T(8,128)(2,1)} %bitcast.187) | data formatting | bytes 3538944 | tf_op jit(solution)/shard_map/reshape | solution.py:98
  471.9 6.0 all-to-all-start.11
  477.9 9.8 %convolution_convert_fusion.5 = bf16[48,48,384]{2,1,0:T(8,128)(2,1)S(1)} fusion(bf16[48,48,384]{2,1,0:T(8,128)(2,1)S(1)} %get-tuple-element.64, bf16[48,384,384]{2,1,0:T(8,128)(2,1)} %all-gather.2.cloned.1.call-done), kind=kOutput, calls=%fused_computation.44 | convolution fusion | flops 680361984 | bytes 17694720 | tf_op jit(solution)/shard_map/sjl,sql->sjq/dot_general | solution.py:91
  487.7 5.4 reshape.298
  493.0 5.4 copy.46
  498.4 7.0 %reshape.299 = bf16[8,96,1152]{2,1,0:T(8,128)(2,1)} reshape(bf16[8,2,48,24,48]{4,3,2,1,0:T(8,128)(2,1)} %bitcast.188) | data formatting | bytes 3538944 | tf_op jit(solution)/shard_map/reshape | solution.py:98
  505.4 11.4 %all-to-all-done.11 = bf16[8,96,1152]{2,1,0:T(8,128)(2,1)} async-done(((bf16[8,96,1152]{2,1,0:T(8,128)(2,1)}), bf16[8,96,1152]{2,1,0:T(8,128)(2,1)}, u32[]{:S(2)}, u32[]{:S(2)}) %all-to-all-start.11) | async-done | bytes 1769504 | tf_op jit(solution)/shard_map/all_to_all | solution.py:43
  516.8 4.5 all-to-all-start.12
  521.3 4.2 fusion.41
  525.6 4.7 reshape.305
  530.3 7.1 %copy.48 = bf16[8,2,48,16,48]{4,0,3,1,2:T(8,128)(2,1)} copy(bf16[8,2,48,16,48]{4,3,2,1,0:T(8,128)(2,1)} %reshape.305) | data formatting | bytes 2359296 | tf_op jit(solution)/shard_map/reshape | solution.py:71
  537.4 5.2 reshape.306
  544.3 10.2 %fusion.12 = (bf16[48,32,384]{2,1,0:T(8,128)(2,1)S(1)}, f32[32,384]{1,0:T(8,128)}, f32[48,32,384]{2,1,0:T(8,128)}) fusion(f32[48,2,1,16,384]{4,3,2,1,0:T(8,128)} %get-tuple-element.50, f32[48,2,1,16,384]{4,3,2,1,0:T(8,128)S(1)} %get-tuple-element.49, f32[32,384]{1,0:T(8,128)S(1)} %bitcast.216, f32[32,384]{1,0:T(8,128)S(1)} %bitcast.215, ...), kind=kOutput, calls=%fused_computation.37 | convolution fusion | flops 457691136 | bytes 23740608 | tf_op jit(solution)/shard_map/sjq,sql->sjl/dot_general | solution.py:73
  555.4 6.5 all-to-all-done.12
  561.9 10.1 %all_to_all.88 = f32[8,6,128]{2,1,0:T(8,128)S(1)} all-to-all(f32[8,6,128]{2,1,0:T(8,128)S(1)} %reshape.307), channel_id=1, replica_groups=mesh['dp'=4,'mp'=8] {'mp'}, dimensions={0} | all-to-all | bytes 49152 | tf_op jit(solution)/shard_map/all_to_all | solution.py:43
  572.6 4.2 all-to-all-start.14
  576.8 10.5 %convolution_convert_fusion.8 = bf16[48,32,384]{2,1,0:T(8,128)(2,1)} fusion(bf16[48,32,384]{2,1,0:T(8,128)(2,1)S(1)} %get-tuple-element.61, bf16[48,384,384]{2,1,0:T(8,128)(2,1)} %all-gather.2.cloned.1.call-done), kind=kOutput, calls=%fused_computation.48 | convolution fusion | flops 453574656 | bytes 16515072 | tf_op jit(solution)/shard_map/sjl,sql->sjq/dot_general | solution.py:91
  587.3 4.2 reshape.303
  593.8 5.5 reshape.304
  599.3 6.1 all-to-all-start.15
  607.0 9.2 %convolution_convert_fusion.11 = bf16[48,16,384]{2,1,0:T(8,128)(2,1)S(1)} fusion(bf16[48,384,384]{2,1,0:T(8,128)(2,1)} %all-gather.2.cloned.1.call-done, f32[48,2,2,8,384]{4,3,2,1,0:T(8,128)S(1)} %bitcast.191, f32[16,384]{1,0:T(8,128)S(1)} %broadcast_bitcast_fusion, f32[16,384]{1,0:T(8,128)S(1)} %broadcast_bitcast_fusion.1, f32[48]{0:T(128)S(1)} %compare_select_fusion), kind=kOutput, calls=%fused_computation.51 | convolution fusion | flops 228261888 | bytes 17154240 | tf_op jit(solution)/shard_map/sjl,sql->sjq/dot_general | solution.py:91
  619.7 13.1 %all-to-all-done.15 = bf16[8,96,768]{2,1,0:T(8,128)(2,1)} async-done(((bf16[8,96,768]{2,1,0:T(8,128)(2,1)}), bf16[8,96,768]{2,1,0:T(8,128)(2,1)}, u32[]{:S(2)}, u32[]{:S(2)}) %all-to-all-start.15) | async-done | bytes 1179680 | tf_op jit(solution)/shard_map/all_to_all | solution.py:43
  632.8 4.4 all-to-all-start.16
  637.3 3.5 convolution_convert_fusion.4
  643.8 3.4 convolution_convert_fusion.7
  647.2 5.4 all-to-all-done.16
  (95 shorter events, 47.7 us)
Async XLA Ops:
  6.5 0.7 copy-start.13
  6.5 239.4 %all-gather.2.cloned.1.call-start = ((), (), s32[]{:S(2)}) async-start(), calls=%async_computation.17 | async-start | bytes 17694720 | tf_op jit(solution)/shard_map/all_gather | solution.py:51
  7.9 14.0 %all-to-all-start = ((s32[8,1,48]{2,1,0:T(1,128)}), s32[8,1,48]{2,1,0:T(1,128)S(1)}, u32[]{:S(2)}, u32[]{:S(2)}) async-start(s32[8,1,48]{2,1,0:T(1,128)} %broadcast_in_dim.22), calls=%async_computation | async-start | bytes 8192 | tf_op jit(solution)/shard_map/all_to_all | solution.py:43
  15.1 4.2 copy-start.2
  27.4 4.4 copy-start.6
  31.8 84.1 %all-to-all-start.1 = ((bf16[8,96,2304]{2,1,0:T(8,128)(2,1)}), bf16[8,96,2304]{2,1,0:T(8,128)(2,1)S(1)}, u32[]{:S(2)}, u32[]{:S(2)}) async-start(bf16[8,96,2304]{2,1,0:T(8,128)(2,1)} %bitcast.196), calls=%async_computation.1 | async-start | bytes 7077888 | tf_op jit(solution)/shard_map/all_to_all | solution.py:43
  115.9 83.1 %all-to-all-start.2 = ((bf16[8,96,2304]{2,1,0:T(8,128)(2,1)}), bf16[8,96,2304]{2,1,0:T(8,128)(2,1)}, u32[]{:S(2)}, u32[]{:S(2)}) async-start(bf16[8,96,2304]{2,1,0:T(8,128)(2,1)} %bitcast.195), calls=%async_computation.2 | async-start | bytes 7077888 | tf_op jit(solution)/shard_map/all_to_all | solution.py:43
  246.0 11.9 %copy-start = (bf16[48,384,384]{2,1,0:T(8,128)(2,1)S(1)}, bf16[48,384,384]{2,1,0:T(8,128)(2,1)}, u32[]{:S(2)}) copy-start(bf16[48,384,384]{2,1,0:T(8,128)(2,1)} %all-gather.2.cloned.1.call-done) | copy-start | bytes 42467332
  257.8 15.0 %copy-start.5 = (bf16[16,48,768]{2,1,0:T(8,128)(2,1)S(1)}, bf16[16,48,768]{2,1,0:T(8,128)(2,1)}, u32[]{:S(2)}) copy-start(bf16[16,48,768]{2,1,0:T(8,128)(2,1)} %get-tuple-element.71) | copy-start | bytes 3538948
  269.2 10.8 %all-to-all-start.3 = ((f32[8,18,128]{2,1,0:T(8,128)}), f32[8,18,128]{2,1,0:T(8,128)S(1)}, u32[]{:S(2)}, u32[]{:S(2)}) async-start(f32[8,18,128]{2,1,0:T(8,128)} %reshape.279), calls=%async_computation.3 | async-start | bytes 196608 | tf_op jit(solution)/shard_map/all_to_all | solution.py:43
  272.8 11.2 %copy-start.7 = (bf16[768,8,2,48]{0,3,2,1:T(8,128)(2,1)S(1)}, bf16[768,8,2,48]{0,3,2,1:T(8,128)(2,1)}, u32[]{:S(2)}) copy-start(bf16[768,8,2,48]{0,3,2,1:T(8,128)(2,1)} %copy-done.6) | copy-start | bytes 3538948
  280.6 10.4 %all-to-all-start.4 = ((f32[8,18,128]{2,1,0:T(8,128)}), f32[8,18,128]{2,1,0:T(8,128)S(1)}, u32[]{:S(2)}, u32[]{:S(2)}) async-start(f32[8,18,128]{2,1,0:T(8,128)} %broadcast_in_dim.23), calls=%async_computation.4 | async-start | bytes 196608 | tf_op jit(solution)/shard_map/all_to_all | solution.py:43
  291.0 0.6 copy-start.11
  291.7 56.4 %all-to-all-start.5 = ((bf16[8,96,1536]{2,1,0:T(8,128)(2,1)}), bf16[8,96,1536]{2,1,0:T(8,128)(2,1)S(1)}, u32[]{:S(2)}, u32[]{:S(2)}) async-start(bf16[8,96,1536]{2,1,0:T(8,128)(2,1)} %bitcast.197), calls=%async_computation.5 | async-start | bytes 4718592 | tf_op jit(solution)/shard_map/all_to_all | solution.py:43
  295.7 1.6 copy-start.8
  348.1 10.8 %all-to-all-start.6 = ((f32[8,18,128]{2,1,0:T(8,128)}), f32[8,18,128]{2,1,0:T(8,128)S(1)}, u32[]{:S(2)}, u32[]{:S(2)}) async-start(f32[8,18,128]{2,1,0:T(8,128)} %reshape.294), calls=%async_computation.6 | async-start | bytes 196608 | tf_op jit(solution)/shard_map/all_to_all | solution.py:43
  359.5 12.4 %all-to-all-start.7 = ((f32[8,18,128]{2,1,0:T(8,128)}), f32[8,18,128]{2,1,0:T(8,128)S(1)}, u32[]{:S(2)}, u32[]{:S(2)}) async-start(f32[8,18,128]{2,1,0:T(8,128)} %broadcast_in_dim.24), calls=%async_computation.7 | async-start | bytes 196608 | tf_op jit(solution)/shard_map/all_to_all | solution.py:43
  371.9 0.6 copy-start.12
  372.5 50.6 %all-to-all-start.8 = ((bf16[8,96,768]{2,1,0:T(8,128)(2,1)}), bf16[8,96,768]{2,1,0:T(8,128)(2,1)S(1)}, u32[]{:S(2)}, u32[]{:S(2)}) async-start(bf16[8,96,768]{2,1,0:T(8,128)(2,1)} %bitcast.209), calls=%async_computation.8 | async-start | bytes 2359296 | tf_op jit(solution)/shard_map/all_to_all | solution.py:43
  423.1 6.5 copy-start.3
  423.1 14.1 %all-to-all-start.9 = ((f32[8,12,128]{2,1,0:T(8,128)}), f32[8,12,128]{2,1,0:T(8,128)S(1)}, u32[]{:S(2)}, u32[]{:S(2)}) async-start(f32[8,12,128]{2,1,0:T(8,128)} %reshape.289), calls=%async_computation.9 | async-start | bytes 131072 | tf_op jit(solution)/shard_map/all_to_all | solution.py:43
  437.9 34.0 %all-to-all-start.10 = ((f32[8,12,128]{2,1,0:T(8,128)}), f32[8,12,128]{2,1,0:T(8,128)}, u32[]{:S(2)}, u32[]{:S(2)}) async-start(f32[8,12,128]{2,1,0:T(8,128)} %broadcast_in_dim.25), calls=%async_computation.10 | async-start | bytes 131072 | tf_op jit(solution)/shard_map/all_to_all | solution.py:43
  471.9 44.9 %all-to-all-start.11 = ((bf16[8,96,1152]{2,1,0:T(8,128)(2,1)}), bf16[8,96,1152]{2,1,0:T(8,128)(2,1)}, u32[]{:S(2)}, u32[]{:S(2)}) async-start(bf16[8,96,1152]{2,1,0:T(8,128)(2,1)} %reshape.284), calls=%async_computation.11 | async-start | bytes 3538944 | tf_op jit(solution)/shard_map/all_to_all | solution.py:43
  516.8 45.1 %all-to-all-start.12 = ((bf16[8,96,1152]{2,1,0:T(8,128)(2,1)}), bf16[8,96,1152]{2,1,0:T(8,128)(2,1)}, u32[]{:S(2)}, u32[]{:S(2)}) async-start(bf16[8,96,1152]{2,1,0:T(8,128)(2,1)} %reshape.299), calls=%async_computation.12 | async-start | bytes 3538944 | tf_op jit(solution)/shard_map/all_to_all | solution.py:43
  521.3 4.3 copy-start.4
  572.6 26.7 %all-to-all-start.14 = ((f32[8,6,128]{2,1,0:T(8,128)}), f32[8,6,128]{2,1,0:T(8,128)}, u32[]{:S(2)}, u32[]{:S(2)}) async-start(f32[8,6,128]{2,1,0:T(8,128)} %broadcast_in_dim.26), calls=%async_computation.14 | async-start | bytes 65536 | tf_op jit(solution)/shard_map/all_to_all | solution.py:43
  599.3 7.7 %copy-start.1 = (f32[48,32,384]{2,1,0:T(8,128)S(1)}, f32[48,32,384]{2,1,0:T(8,128)}, u32[]{:S(2)}) copy-start(f32[48,32,384]{2,1,0:T(8,128)} %get-tuple-element.68) | copy-start | bytes 7077892
  599.3 33.5 %all-to-all-start.15 = ((bf16[8,96,768]{2,1,0:T(8,128)(2,1)}), bf16[8,96,768]{2,1,0:T(8,128)(2,1)}, u32[]{:S(2)}, u32[]{:S(2)}) async-start(bf16[8,96,768]{2,1,0:T(8,128)(2,1)} %reshape.304), calls=%async_computation.15 | async-start | bytes 2359296 | tf_op jit(solution)/shard_map/all_to_all | solution.py:43
  632.8 19.9 %all-to-all-start.16 = ((bf16[8,96,384]{2,1,0:T(8,128)(2,1)}), bf16[8,96,384]{2,1,0:T(8,128)(2,1)}, u32[]{:S(2)}, u32[]{:S(2)}) async-start(bf16[8,96,384]{2,1,0:T(8,128)(2,1)} %reshape.312), calls=%async_computation.16 | async-start | bytes 1179648 | tf_op jit(solution)/shard_map/all_to_all | solution.py:43
  637.3 3.5 copy-start.9
  652.7 2.2 copy-start.10
Sparse Core Ops, SparseCore 0:
  8.9 93.7 all-gather.1

commit v3 on v2

--- a/solution.py
+++ b/solution.py
@@ -6,25 +6,16 @@
 from jax.sharding import PartitionSpec as P
 
 MERIDIAN_POINTS = 768
-CUTS = (0, 3, 6, 8, 9)
 
 
-def transform_table(orders, blocks):
+def transform_table(orders):
     longitude = jnp.arange(MERIDIAN_POINTS, dtype=jnp.int32)
     phase_index = longitude[:, None] * orders[None, :] % MERIDIAN_POINTS
     radians = phase_index.astype(jnp.float32) * (2.0 * math.pi / MERIDIAN_POINTS)
     norm_factor = 1.0 / math.sqrt(MERIDIAN_POINTS)
-    cosine = (jnp.cos(radians) * norm_factor).astype(jnp.bfloat16)
-    sine = (-jnp.sin(radians) * norm_factor).astype(jnp.bfloat16)
-    slots = orders.shape[0] // blocks
-    both = jnp.stack(
-        [
-            cosine.reshape(MERIDIAN_POINTS, blocks, slots),
-            sine.reshape(MERIDIAN_POINTS, blocks, slots),
-        ],
-        axis=2,
-    )
-    return both.reshape(MERIDIAN_POINTS, 2 * orders.shape[0])
+    return jnp.stack(
+        [jnp.cos(radians) * norm_factor, -jnp.sin(radians) * norm_factor], axis=1
+    ).astype(jnp.bfloat16)
 
 
 def local(
@@ -51,7 +42,9 @@
     full_table = lax.all_gather(associated_function_table, "dp", axis=1, tiled=True)
     latitudes, degrees = full_table.shape[1:]
     orders = share(zonal_wavenumber_map[None]).reshape(blocks * slots)
-    fourier = transform_table(orders, blocks)
+    by_part = transform_table(orders)
+    fourier = by_part.reshape(MERIDIAN_POINTS, 2, blocks, slots).transpose(0, 2, 1, 3)
+    fourier = fourier.reshape(MERIDIAN_POINTS, 2 * blocks * slots)
     order_weight = jnp.where(zonal_wavenumber_map == 0, 1.0, 2.0).astype(jnp.float32)
     magnitude, phase = magnitude_factor.T, phase_match_factor.T
 
@@ -64,15 +57,28 @@
             (((0,), (1,)), ((), ())),
             preferred_element_type=jnp.float32,
         ).astype(jnp.bfloat16)
-        return exchange(spec.reshape(blocks, 2 * slots, 2 * part * lat_dev))
+        return spec.reshape(blocks, 2 * slots, 2 * part * lat_dev)
 
-    def analyse(spec, rows):
+    def to_slots_wide(rows):
         part = rows.stop - rows.start
-        spec = spec.reshape(blocks, 2, slots, 2 * part, lat_dev)
-        spec = spec.transpose(2, 1, 3, 0, 4).reshape(slots, 4 * part, latitudes)
-        coef = jnp.einsum("sjq,sql->sjl", spec, full_table, preferred_element_type=jnp.float32)
+        both = [
+            jnp.einsum(
+                "cqn,nkm->mqkc", fields[0, rows], by_part, preferred_element_type=jnp.float32
+            ).astype(jnp.bfloat16)
+            for fields in (prediction_maps, observed_maps)
+        ]
+        spec = jnp.stack(both, axis=2)
+        return spec.reshape(blocks, slots, lat_dev, 4 * part)
+
+    def narrow_lines(spec, rows):
+        part = rows.stop - rows.start
+        spec = spec.reshape(blocks, 2, slots, 2, part, lat_dev)
+        return spec.transpose(2, 3, 1, 4, 0, 5).reshape(slots, 4 * part, latitudes)
+
+    def analyse(coef, rows):
+        part = rows.stop - rows.start
         coef = coef.reshape(slots, 2, 2, part, degrees)
-        return coef, jnp.sum(order_weight[:, None, None, None, None] * coef * coef, axis=(0, 1))
+        return coef, jnp.sum(order_weight[:, None, None, None, None] * coef * coef, axis=(0, 2))
 
     def sum_orders(power):
         width = math.gcd(128, power.size // blocks)
@@ -86,7 +92,7 @@
         true_factor = -2.0 * phase[rows]
         grad_coef = (
             order_weight[:, None, None, None]
-            * (pred_factor * coef[:, :, 0] + true_factor * coef[:, :, 1])
+            * (pred_factor * coef[:, 0] + true_factor * coef[:, 1])
         ).astype(jnp.bfloat16)
         grad_spec = jnp.einsum(
             "sjl,sql->sjq",
@@ -107,32 +113,47 @@
         ).astype(jnp.bfloat16)
         return grad_grid.reshape(part, lat_dev, MERIDIAN_POINTS)
 
-    bounds = [channels * cut // 9 for cut in CUTS]
-    groups = [slice(low, high) for low, high in zip(bounds[:-1], bounds[1:])]
-    count = len(groups)
-    spec, coef, power, grad, results = {}, {}, {}, {}, {}
+    narrow = channels // 9
+    middle = (channels + narrow) // 2
+    groups = [slice(0, narrow), slice(narrow, middle), slice(middle, channels)]
 
-    def forward(group):
-        spec[group] = to_slots(groups[group])
+    def after(array):
+        return lax.optimization_barrier((array, last[0]))[0]
 
-    def legendre(group):
-        coef[group], partial = analyse(spec[group], groups[group])
-        power[group] = sum_orders(partial)
-        grad[group] = synthesise(coef[group], power[group], groups[group])
+    def legendre_narrow(spec):
+        return jnp.einsum(
+            "sjq,sql->sjl",
+            narrow_lines(spec, groups[0]),
+            full_table,
+            preferred_element_type=jnp.float32,
+        )
 
-    def backward(group):
-        results[group] = to_grid(grad[group], groups[group])
+    def legendre_wide(spec, table):
+        lines = spec.transpose(1, 0, 2, 3).reshape(table.shape[0], latitudes, spec.shape[3])
+        return jnp.einsum("sqj,sql->sjl", lines, table, preferred_element_type=jnp.float32)
 
-    forward(0)
-    for group in range(1, count):
-        forward(group)
-        legendre(group - 1)
-    for group in range(count - 2):
-        backward(group)
-    legendre(count - 1)
-    backward(count - 2)
-    backward(count - 1)
-    return jnp.concatenate([results[group] for group in range(count)], axis=0)[None]
+    half = slots // 2
+    spec_0 = exchange(to_slots(groups[0]))
+    spec_1 = exchange(to_slots_wide(groups[1]))
+    coef_0, partial_0 = analyse(legendre_narrow(spec_0), groups[0])
+    payload_2 = to_slots_wide(groups[2])
+    power_0 = sum_orders(partial_0)
+    spec_1 = after(spec_1)
+    low_2 = exchange(payload_2[:, :half])
+    coef_1, partial_1 = analyse(legendre_wide(spec_1, full_table), groups[1])
+    power_1 = sum_orders(partial_1)
+    coef_0, coef_1 = after((coef_0, coef_1))
+    high_2 = exchange(payload_2[:, half:])
+    grad_0 = synthesise(coef_0, power_0, groups[0])
+    grad_1 = synthesise(coef_1, power_1, groups[1])
+    result_0 = to_grid(grad_0, groups[0])
+    spec_2 = jnp.concatenate([low_2, high_2], axis=1)
+    coef_2, partial_2 = analyse(legendre_wide(spec_2, full_table), groups[2])
+    power_2 = sum_orders(partial_2)
+    coef_2 = after(coef_2)
+    result_1 = to_grid(grad_1, groups[1])
+    result_2 = to_grid(synthesise(coef_2, power_2, groups[2]), groups[2])
+    return jnp.concatenate([result_0, result_1, result_2], axis=0)[None]
 
 
 def solution(mesh):

time: 674 us -> 635 us (0.942)
  starting transfers between devices: 80.9 us -> 57.6 us
  local copies, waits for them, and re-layouts: 223 us -> 202 us
  matrix products: 114 us -> 97.4 us
  waiting for transfers between devices: 194 us -> 207 us
  blocking collectives: 10.1 us -> 20.1 us
    reshape x12 -> x5, local copies, waits for them, and re-layouts: 138 us -> 48.6 us  [the longest x2 34.3 us: to_slots_wide(): return spec.reshape(blocks, slots, lat_dev, 4 * part)]
    optimization_barrier x0 -> x4, local copies, waits for them, and re-layouts: none -> 39.8 us  [the longest x3 36.1 us: exchange(): array, _ = lax.optimization_barrier((array, last[0]))]
    all_to_all x16 -> x12, starting transfers between devices: 80.9 us -> 57.6 us  [exchange(): lax.all_to_all(array, 'mp', split_axis=0, concat_axis=0, tiled=True)]
    dot_general x4 -> x1, matrix products: 18.8 us -> 2.13 us  [to_slots(): lax.dot_general(fourier, grid.reshape(2 * part * lat_dev, MERIDIAN_POINTS...]
    slice x3, local copies, waits for them, and re-layouts: 17.1 us -> 33.1 us  [the longest x1 19.1 us: local(): low_2 = exchange(payload_2[:, :half])]
    another operation x1 -> x5, other arithmetic: 0.11 us -> 13.3 us  [transform_table(): jnp.stack([cosine.reshape(MERIDIAN_POINTS, blocks, slots), sine.reshape(M...]
    all_to_all x16 -> x12, waiting for transfers between devices: 193 us -> 206 us  [exchange(): lax.all_to_all(array, 'mp', split_axis=0, concat_axis=0, tiled=True)]
    dot_general x4 -> x7, matrix products: 43.2 us -> 53.3 us  [the longest x2 26.2 us: legendre_wide(): jnp.einsum('sqj,sql->sjl', lines, table, preferred_element_type=jnp.float32)]
  transfers between devices with their start and end apart: 17 -> 13, of which waited for: 11 -> 9; matrix products, arithmetic and copies ran while one was open for 50% -> 39% of each run, Pallas kernels for 0% -> 0%
where the time goes in v3:
time: 635 us; the launch traced here: 623 us
  waiting for transfers between devices  207 us (33%)
  local copies, waits for them, and re-layouts  202 us (32%)
  matrix products  97.4 us (15%)
  starting transfers between devices  57.6 us (9%)
  other arithmetic  25.3 us (4%)
  blocking collectives  20.1 us (3%)
  between operations  14.3 us (2%)
    all_to_all x12, waiting for transfers between devices, exchange(): lax.all_to_all(array, 'mp', split_axis=0, concat_axis=0, tiled=True)  206 us
    all_to_all x12, starting transfers between devices, exchange(): lax.all_to_all(array, 'mp', split_axis=0, concat_axis=0, tiled=True)  57.6 us
    optimization_barrier x3, local copies, waits for them, and re-layouts, exchange(): array, _ = lax.optimization_barrier((array, last[0]))  36.1 us
    reshape x6, local copies, waits for them, and re-layouts, synthesise(): grad_spec.reshape(slots, 2, part, blocks, lat_dev).transpose(3, 1, 0, 2, 4)  34.6 us
    reshape x2, local copies, waits for them, and re-layouts, to_slots_wide(): return spec.reshape(blocks, slots, lat_dev, 4 * part)  34.3 us
    dot_general x3, matrix products, synthesise(): jnp.einsum('sjl,sql->sjq', grad_coef.reshape(slots, 2 * part, degrees), f...  32.3 us
    reshape x3, local copies, waits for them, and re-layouts, synthesise(): return grad_spec.reshape(blocks, 2 * slots, part * lat_dev)  28.7 us
    dot_general x2, matrix products, legendre_wide(): jnp.einsum('sqj,sql->sjl', lines, table, preferred_element_type=jnp.float32)  26.2 us
  transfers between devices with their start and end apart: 13, of which 9 were waited for; matrix products, arithmetic and copies ran while one was open for 39% of the time, Pallas kernels for 0%

profile of v3, /device:TPU:0, one launch (start us, length us, event | category | flops | bytes accessed | tf_op | source)
XLA Modules:
  0.0 623.1 jit_solution(4451673909328486129)
XLA Ops:
  7.9 7.3 %all-to-all-start = ((s32[8,1,48]{2,1,0:T(1,128)}), s32[8,1,48]{2,1,0:T(1,128)S(1)}, u32[]{:S(2)}, u32[]{:S(2)}) async-start(s32[8,1,48]{2,1,0:T(1,128)} %broadcast_in_dim.20), calls=%async_computation | async-start | bytes 8192 | tf_op jit(solution)/shard_map/all_to_all | solution.py:34
  16.6 5.0 all-to-all-done
  21.5 5.4 multiply_convert_fusion.3
  27.1 2.1 convolution_convert_fusion.4
  29.2 3.6 all-to-all-start.1
  34.0 5.1 multiply_convert_fusion.1
  39.1 3.7 convert_bitcast_fusion.2
  42.8 3.7 convert_bitcast_fusion.3
  47.0 3.4 copy.34
  50.3 17.1 %reshape.302 = bf16[8,48,48,128]{1,0,3,2:T(8,128)(2,1)} reshape(bf16[384,48,2,2,32]{0,4,3,2,1:T(8,128)(2,1)} %copy.34) | data formatting | bytes 9437184 | tf_op jit(solution)/shard_map/reshape | solution.py:71
  67.5 12.8 %copy.35 = bf16[8,48,48,128]{3,2,1,0:T(8,128)(2,1)} copy(bf16[8,48,48,128]{1,0,3,2:T(8,128)(2,1)} %reshape.302) | data formatting | bytes 9437184 | tf_op jit(solution)/shard_map/optimization_barrier | solution.py:33
  80.3 6.1 all-to-all-start.2
  86.4 5.1 convert_bitcast_fusion
  91.5 5.3 convert_bitcast_fusion.1
  96.8 4.7 reshape.299
  101.4 5.3 copy.55
  106.7 4.4 reshape.300
  111.2 9.4 %fusion.8 = (f32[32,384]{1,0:T(8,128)}, f32[48,32,384]{2,1,0:T(8,128)}) fusion(f32[48]{0:T(128)S(1)} %compare_select_fusion, bf16[48,32,384]{2,1,0:T(8,128)(2,1)S(1)} %reshape.300, bf16[48,384,384]{2,1,0:T(8,128)(2,1)} %all-gather.2.cloned.1.call-done), kind=kOutput, calls=%fused_computation.24 | convolution fusion | flops 454742016 | bytes 17744064 | tf_op jit(solution)/shard_map/sjq,sql->sjl/dot_general | solution.py:124
  122.0 67.1 %all-to-all-done.2 = bf16[8,48,48,128]{3,2,1,0:T(8,128)(2,1)} async-done(((bf16[8,48,48,128]{3,2,1,0:T(8,128)(2,1)}), bf16[8,48,48,128]{3,2,1,0:T(8,128)(2,1)}, u32[]{:S(2)}, u32[]{:S(2)}) %all-to-all-start.2) | async-done | bytes 4718624 | tf_op jit(solution)/shard_map/all_to_all | solution.py:34
  189.1 4.1 all-to-all-start.3
  193.2 2.2 pad_maximum_fusion.1
  195.4 3.4 copy.38
  198.8 17.1 %reshape.307 = bf16[8,48,48,128]{1,0,3,2:T(8,128)(2,1)} reshape(bf16[384,48,2,2,32]{0,4,3,2,1:T(8,128)(2,1)} %copy.38) | data formatting | bytes 9437184 | tf_op jit(solution)/shard_map/reshape | solution.py:71
  216.5 6.0 all-to-all-start.4
  222.5 19.1 %fusion.55 = (bf16[8,24,48,128]{1,0,3,2:T(8,128)(2,1)}, bf16[8,24,48,128]{1,0,3,2:T(8,128)(2,1)}) fusion(bf16[8,48,48,128]{1,0,3,2:T(8,128)(2,1)} %reshape.307), kind=kLoop, calls=%fused_computation.102 | loop fusion | bytes 9437184 | tf_op jit(solution)/shard_map/slice | solution.py:142
  241.6 11.6 %copy.39 = bf16[8,24,48,128]{3,2,1,0:T(8,128)(2,1)} copy(bf16[8,24,48,128]{1,0,3,2:T(8,128)(2,1)} %get-tuple-element.29) | data formatting | bytes 4718592 | tf_op jit(solution)/shard_map/optimization_barrier | solution.py:33
  253.2 6.0 all-to-all-start.5
  259.2 3.7 copy.36
  262.9 12.5 %fusion = (f32[128,384]{1,0:T(8,128)S(1)}, f32[48,128,384]{2,1,0:T(8,128)}) fusion(f32[48]{0:T(128)S(1)} %compare_select_fusion, bf16[48,384,128]{2,1,0:T(8,128)(2,1)S(1)} %bitcast.176, bf16[48,384,384]{2,1,0:T(8,128)(2,1)} %all-gather.2.cloned.1.call-done), kind=kOutput, calls=%fused_computation.2 | convolution fusion | flops 1818968064 | bytes 28508352 | tf_op jit(solution)/shard_map/sqj,sql->sjl/dot_general | solution.py:133
  275.4 36.7 %all-to-all-done.5 = bf16[8,24,48,128]{3,2,1,0:T(8,128)(2,1)S(1)} async-done(((bf16[8,24,48,128]{3,2,1,0:T(8,128)(2,1)}), bf16[8,24,48,128]{3,2,1,0:T(8,128)(2,1)S(1)}, u32[]{:S(2)}, u32[]{:S(2)}) %all-to-all-start.5) | async-done | bytes 2359328 | tf_op jit(solution)/shard_map/all_to_all | solution.py:34
  312.1 10.5 %all_to_all.70 = f32[8,24,128]{2,1,0:T(8,128)S(1)} all-to-all(f32[8,24,128]{2,1,0:T(8,128)S(1)} %reshape.306), channel_id=1, replica_groups=mesh['dp'=4,'mp'=8] {'mp'}, dimensions={0} | all-to-all | bytes 196608 | tf_op jit(solution)/shard_map/all_to_all | solution.py:34
  322.7 9.5 %all_to_all.71 = f32[8,24,128]{2,1,0:T(8,128)S(1)} all-to-all(f32[8,24,128]{2,1,0:T(8,128)S(1)} %broadcast_in_dim.22), channel_id=1, replica_groups=mesh['dp'=4,'mp'=8] {'mp'}, dimensions={0} | all-to-all | bytes 196608 | tf_op jit(solution)/shard_map/all_to_all | solution.py:34
  332.2 11.7 %copy.41 = bf16[8,24,48,128]{3,2,1,0:T(8,128)(2,1)} copy(bf16[8,24,48,128]{1,0,3,2:T(8,128)(2,1)} %get-tuple-element.33) | data formatting | bytes 4718592 | tf_op jit(solution)/shard_map/optimization_barrier | solution.py:33
  343.9 4.7 all-to-all-start.8
  348.7 10.0 %convolution_convert_fusion.6 = bf16[48,16,384]{2,1,0:T(8,128)(2,1)S(1)} fusion(bf16[48,384,384]{2,1,0:T(8,128)(2,1)} %all-gather.2.cloned.1.call-done, f32[48,2,2,8,384]{4,3,2,1,0:T(8,128)} %bitcast.184, f32[16,384]{1,0:T(8,128)S(1)} %broadcast_bitcast_fusion, f32[16,384]{1,0:T(8,128)S(1)} %broadcast_bitcast_fusion.1, f32[48]{0:T(128)S(1)} %compare_select_fusion), kind=kOutput, calls=%fused_computation.48 | convolution fusion | flops 228261888 | bytes 17154240 | tf_op jit(solution)/shard_map/sjl,sql->sjq/dot_general | solution.py:97
  358.7 2.2 reshape.308
  360.9 2.9 copy.56
  363.8 3.2 reshape.309
  367.0 9.2 %fusion.56 = (f32[48,1,2,32,384]{4,3,2,1,0:T(8,128)}, f32[48,1,2,32,384]{4,3,2,1,0:T(8,128)}) fusion(f32[48,2,2,32,384]{4,3,2,1,0:T(8,128)} %bitcast.173), kind=kLoop, calls=%fused_computation.103 | loop fusion | bytes 18874368 | tf_op jit(solution)/shard_map/slice | solution.py:95
  376.2 24.3 %all-to-all-done.8 = bf16[8,24,48,128]{3,2,1,0:T(8,128)(2,1)} async-done(((bf16[8,24,48,128]{3,2,1,0:T(8,128)(2,1)}), bf16[8,24,48,128]{3,2,1,0:T(8,128)(2,1)}, u32[]{:S(2)}, u32[]{:S(2)}) %all-to-all-start.8) | async-done | bytes 2359328 | tf_op jit(solution)/shard_map/all_to_all | solution.py:34
  402.5 3.5 copy.43
  406.1 3.5 all-to-all-start.9
  409.6 13.7 %fusion.1 = (f32[128,384]{1,0:T(8,128)S(1)}, f32[48,128,384]{2,1,0:T(8,128)}) fusion(f32[48]{0:T(128)S(1)} %compare_select_fusion, bf16[48,384,128]{2,1,0:T(8,128)(2,1)} %bitcast.175, bf16[48,384,384]{2,1,0:T(8,128)(2,1)} %all-gather.2.cloned.1.call-done), kind=kOutput, calls=%fused_computation.3 | convolution fusion | flops 1818968064 | bytes 28508352 | tf_op jit(solution)/shard_map/sqj,sql->sjl/dot_general | solution.py:133
  425.6 4.4 all-to-all-start.10
  430.0 7.1 %all-to-all-done.10 = f32[8,24,128]{2,1,0:T(8,128)S(1)} async-done(((f32[8,24,128]{2,1,0:T(8,128)}), f32[8,24,128]{2,1,0:T(8,128)S(1)}, u32[]{:S(2)}, u32[]{:S(2)}) %all-to-all-start.10) | async-done | bytes 98336 | tf_op jit(solution)/shard_map/all_to_all | solution.py:34
  437.8 3.6 all-to-all-start.11
  441.4 7.0 %all-to-all-done.11 = f32[8,24,128]{2,1,0:T(8,128)S(1)} async-done(((f32[8,24,128]{2,1,0:T(8,128)}), f32[8,24,128]{2,1,0:T(8,128)S(1)}, u32[]{:S(2)}, u32[]{:S(2)}) %all-to-all-start.11) | async-done | bytes 98336 | tf_op jit(solution)/shard_map/all_to_all | solution.py:34
  448.5 4.9 fusion.57
  454.9 5.4 fusion.7
  460.2 10.8 %convolution_convert_fusion.3 = bf16[48,64,384]{2,1,0:T(8,128)(2,1)S(1)} fusion(bf16[48,64,384]{2,1,0:T(8,128)(2,1)} %get-tuple-element.57, bf16[48,384,384]{2,1,0:T(8,128)(2,1)} %all-gather.2.cloned.1.call-done), kind=kOutput, calls=%fused_computation.42 | convolution fusion | flops 907149312 | bytes 18874368 | tf_op jit(solution)/shard_map/sjl,sql->sjq/dot_general | solution.py:97
  471.1 7.0 %reshape.312 = bf16[48,2,32,8,48]{4,3,2,1,0:T(8,128)(2,1)} reshape(bf16[48,64,384]{2,1,0:T(8,128)(2,1)S(1)} %convolution_convert_fusion.3) | data formatting | bytes 4718592 | tf_op jit(solution)/shard_map/reshape | solution.py:103
  478.1 6.6 %copy.54 = bf16[48,2,32,8,48]{4,2,0,1,3:T(8,128)(2,1)} copy(bf16[48,2,32,8,48]{4,3,2,1,0:T(8,128)(2,1)} %reshape.312) | data formatting | bytes 4718592 | tf_op jit(solution)/shard_map/reshape | solution.py:103
  484.6 12.8 %reshape.313 = bf16[8,96,1536]{2,1,0:T(8,128)(2,1)} reshape(bf16[8,2,48,32,48]{4,3,2,1,0:T(8,128)(2,1)} %bitcast.177) | data formatting | bytes 4718592 | tf_op jit(solution)/shard_map/reshape | solution.py:104
  497.4 4.8 all-to-all-start.12
  502.2 11.5 %convolution_convert_fusion.2 = bf16[48,64,384]{2,1,0:T(8,128)(2,1)} fusion(bf16[48,64,384]{2,1,0:T(8,128)(2,1)S(1)} %copy-done, bf16[48,384,384]{2,1,0:T(8,128)(2,1)} %all-gather.2.cloned.1.call-done), kind=kOutput, calls=%fused_computation.41 | convolution fusion | flops 907149312 | bytes 18874368 | tf_op jit(solution)/shard_map/sjl,sql->sjq/dot_general | solution.py:97
  513.7 9.2 %reshape.319 = bf16[48,2,32,8,48]{4,3,2,1,0:T(8,128)(2,1)} reshape(bf16[48,64,384]{2,1,0:T(8,128)(2,1)} %convolution_convert_fusion.2) | data formatting | bytes 4718592 | tf_op jit(solution)/shard_map/reshape | solution.py:103
  522.9 6.6 %copy.53 = bf16[48,2,32,8,48]{4,2,0,1,3:T(8,128)(2,1)} copy(bf16[48,2,32,8,48]{4,3,2,1,0:T(8,128)(2,1)} %reshape.319) | data formatting | bytes 4718592 | tf_op jit(solution)/shard_map/reshape | solution.py:103
  529.5 12.8 %reshape.320 = bf16[8,96,1536]{2,1,0:T(8,128)(2,1)} reshape(bf16[8,2,48,32,48]{4,3,2,1,0:T(8,128)(2,1)} %bitcast.178) | data formatting | bytes 4718592 | tf_op jit(solution)/shard_map/reshape | solution.py:104
  542.3 11.2 %all-to-all-done.12 = bf16[8,96,1536]{2,1,0:T(8,128)(2,1)} async-done(((bf16[8,96,1536]{2,1,0:T(8,128)(2,1)}), bf16[8,96,1536]{2,1,0:T(8,128)(2,1)}, u32[]{:S(2)}, u32[]{:S(2)}) %all-to-all-start.12) | async-done | bytes 2359328 | tf_op jit(solution)/shard_map/all_to_all | solution.py:34
  553.5 3.6 all-to-all-start.13
  557.1 2.6 convolution_convert_fusion.5
  559.7 5.1 convolution_convert_fusion.1
  564.8 46.2 %all-to-all-done.13 = bf16[8,96,1536]{2,1,0:T(8,128)(2,1)S(1)} async-done(((bf16[8,96,1536]{2,1,0:T(8,128)(2,1)}), bf16[8,96,1536]{2,1,0:T(8,128)(2,1)S(1)}, u32[]{:S(2)}, u32[]{:S(2)}) %all-to-all-start.13) | async-done | bytes 2359328 | tf_op jit(solution)/shard_map/all_to_all | solution.py:34
  613.0 2.8 maximum_bitcast_fusion
  (79 shorter events, 15.4 us)
Async XLA Ops:
  6.5 0.7 copy-start.10
  6.5 104.6 %all-gather.2.cloned.1.call-start = ((), (), s32[]{:S(2)}) async-start(), calls=%async_computation.14 | async-start | bytes 17694720 | tf_op jit(solution)/shard_map/all_gather | solution.py:42
  7.9 13.6 %all-to-all-start = ((s32[8,1,48]{2,1,0:T(1,128)}), s32[8,1,48]{2,1,0:T(1,128)S(1)}, u32[]{:S(2)}, u32[]{:S(2)}) async-start(s32[8,1,48]{2,1,0:T(1,128)} %broadcast_in_dim.20), calls=%async_computation | async-start | bytes 8192 | tf_op jit(solution)/shard_map/all_to_all | solution.py:34
  27.0 2.1 copy-start.4
  29.2 38.3 %all-to-all-start.1 = ((bf16[8,96,768]{2,1,0:T(8,128)(2,1)}), bf16[8,96,768]{2,1,0:T(8,128)(2,1)S(1)}, u32[]{:S(2)}, u32[]{:S(2)}) async-start(bf16[8,96,768]{2,1,0:T(8,128)(2,1)} %bitcast.7), calls=%async_computation.1 | async-start | bytes 2359296 | tf_op jit(solution)/shard_map/all_to_all | solution.py:34
  67.5 12.8 %copy-start.1 = (bf16[8,96,768]{2,1,0:T(8,128)(2,1)}, bf16[8,96,768]{2,1,0:T(8,128)(2,1)S(1)}, u32[]{:S(2)}) copy-start(bf16[8,96,768]{2,1,0:T(8,128)(2,1)S(1)} %all-to-all-done.1) | copy-start | bytes 3538948
  80.3 108.8 %all-to-all-start.2 = ((bf16[8,48,48,128]{3,2,1,0:T(8,128)(2,1)}), bf16[8,48,48,128]{3,2,1,0:T(8,128)(2,1)}, u32[]{:S(2)}, u32[]{:S(2)}) async-start(bf16[8,48,48,128]{3,2,1,0:T(8,128)(2,1)} %copy.35), calls=%async_computation.2 | async-start | bytes 9437184 | tf_op jit(solution)/shard_map/all_to_all | solution.py:34
  111.1 82.1 %copy-start.2 = (bf16[384,48,1,2,32]{0,1,4,3,2:T(8,128)(2,1)S(1)}, bf16[384,48,1,2,32]{0,1,4,3,2:T(8,128)(2,1)}, u32[]{:S(2)}) copy-start(bf16[384,48,1,2,32]{0,1,4,3,2:T(8,128)(2,1)} %convert_bitcast_fusion) | copy-start | bytes 7077892
  189.1 26.8 %all-to-all-start.3 = ((f32[8,6,128]{2,1,0:T(8,128)}), f32[8,6,128]{2,1,0:T(8,128)S(1)}, u32[]{:S(2)}, u32[]{:S(2)}) async-start(f32[8,6,128]{2,1,0:T(8,128)} %reshape.301), calls=%async_computation.3 | async-start | bytes 65536 | tf_op jit(solution)/shard_map/all_to_all | solution.py:34
  216.5 25.1 %all-to-all-start.4 = ((f32[8,6,128]{2,1,0:T(8,128)}), f32[8,6,128]{2,1,0:T(8,128)S(1)}, u32[]{:S(2)}, u32[]{:S(2)}) async-start(f32[8,6,128]{2,1,0:T(8,128)} %broadcast_in_dim.21), calls=%async_computation.4 | async-start | bytes 65536 | tf_op jit(solution)/shard_map/all_to_all | solution.py:34
  253.2 58.9 %all-to-all-start.5 = ((bf16[8,24,48,128]{3,2,1,0:T(8,128)(2,1)}), bf16[8,24,48,128]{3,2,1,0:T(8,128)(2,1)S(1)}, u32[]{:S(2)}, u32[]{:S(2)}) async-start(bf16[8,24,48,128]{3,2,1,0:T(8,128)(2,1)} %copy.39), calls=%async_computation.5 | async-start | bytes 4718592 | tf_op jit(solution)/shard_map/all_to_all | solution.py:34
  343.9 4.7 copy-start.8
  343.9 4.8 copy-start.9
  343.9 56.6 %all-to-all-start.8 = ((bf16[8,24,48,128]{3,2,1,0:T(8,128)(2,1)}), bf16[8,24,48,128]{3,2,1,0:T(8,128)(2,1)}, u32[]{:S(2)}, u32[]{:S(2)}) async-start(bf16[8,24,48,128]{3,2,1,0:T(8,128)(2,1)} %copy.41), calls=%async_computation.8 | async-start | bytes 4718592 | tf_op jit(solution)/shard_map/all_to_all | solution.py:34
  406.1 19.5 %all-to-all-start.9 = ((bf16[8,96,384]{2,1,0:T(8,128)(2,1)}), bf16[8,96,384]{2,1,0:T(8,128)(2,1)S(1)}, u32[]{:S(2)}, u32[]{:S(2)}) async-start(bf16[8,96,384]{2,1,0:T(8,128)(2,1)} %reshape.309), calls=%async_computation.9 | async-start | bytes 1179648 | tf_op jit(solution)/shard_map/all_to_all | solution.py:34
  425.6 22.9 %copy-start.6 = (bf16[8,96,384]{2,1,0:T(8,128)(2,1)}, bf16[8,96,384]{2,1,0:T(8,128)(2,1)S(1)}, u32[]{:S(2)}) copy-start(bf16[8,96,384]{2,1,0:T(8,128)(2,1)S(1)} %all-to-all-done.9) | copy-start | bytes 1769476
  425.6 11.5 %all-to-all-start.10 = ((f32[8,24,128]{2,1,0:T(8,128)}), f32[8,24,128]{2,1,0:T(8,128)S(1)}, u32[]{:S(2)}, u32[]{:S(2)}) async-start(f32[8,24,128]{2,1,0:T(8,128)} %reshape.315), calls=%async_computation.10 | async-start | bytes 196608 | tf_op jit(solution)/shard_map/all_to_all | solution.py:34
  437.8 10.6 %all-to-all-start.11 = ((f32[8,24,128]{2,1,0:T(8,128)}), f32[8,24,128]{2,1,0:T(8,128)S(1)}, u32[]{:S(2)}, u32[]{:S(2)}) async-start(f32[8,24,128]{2,1,0:T(8,128)} %broadcast_in_dim.23), calls=%async_computation.11 | async-start | bytes 196608 | tf_op jit(solution)/shard_map/all_to_all | solution.py:34
  448.5 5.0 slice-start
  448.5 6.2 slice-start.2
  448.5 6.2 %slice-start.1 = ((s8[4718592]{0:T(1024)(128)(4,1)}), s8[524288]{0:T(1024)(128)(4,1)S(1)}, s32[]{:S(2)}) async-start(s8[4718592]{0:T(1024)(128)(4,1)} %bitcast.179), calls=%async_computation.16 | async-start | bytes 1048576
  448.5 6.4 %slice-start.3 = ((s8[4718592]{0:T(1024)(128)(4,1)}), s8[524288]{0:T(1024)(128)(4,1)S(1)}, s32[]{:S(2)}) async-start(s8[4718592]{0:T(1024)(128)(4,1)} %bitcast.181), calls=%async_computation.18 | async-start | bytes 1048576
  497.4 4.8 copy-start
  497.4 56.1 %all-to-all-start.12 = ((bf16[8,96,1536]{2,1,0:T(8,128)(2,1)}), bf16[8,96,1536]{2,1,0:T(8,128)(2,1)}, u32[]{:S(2)}, u32[]{:S(2)}) async-start(bf16[8,96,1536]{2,1,0:T(8,128)(2,1)} %reshape.313), calls=%async_computation.12 | async-start | bytes 4718592 | tf_op jit(solution)/shard_map/all_to_all | solution.py:34
  542.3 14.8 %copy-start.5 = (bf16[768,2,8,48]{0,3,1,2:T(8,128)(2,1)S(1)}, bf16[768,2,8,48]{0,3,1,2:T(8,128)(2,1)}, u32[]{:S(2)}) copy-start(bf16[768,2,8,48]{0,3,1,2:T(8,128)(2,1)} %copy-done.4) | copy-start | bytes 3538948
  553.5 57.5 %all-to-all-start.13 = ((bf16[8,96,1536]{2,1,0:T(8,128)(2,1)}), bf16[8,96,1536]{2,1,0:T(8,128)(2,1)S(1)}, u32[]{:S(2)}, u32[]{:S(2)}) async-start(bf16[8,96,1536]{2,1,0:T(8,128)(2,1)} %reshape.320), calls=%async_computation.13 | async-start | bytes 4718592 | tf_op jit(solution)/shard_map/all_to_all | solution.py:34
  611.0 2.1 copy-start.3
  611.0 2.1 copy-start.7
Sparse Core Ops, SparseCore 0:
  8.9 93.7 all-gather.1

commit v4 on v3

--- a/solution.py
+++ b/solution.py
@@ -3,6 +3,7 @@
 import jax
 import jax.numpy as jnp
 from jax import lax
+from jax.experimental.layout import Layout, with_layout_constraint
 from jax.sharding import PartitionSpec as P
 
 MERIDIAN_POINTS = 768
@@ -59,16 +60,17 @@
         ).astype(jnp.bfloat16)
         return spec.reshape(blocks, 2 * slots, 2 * part * lat_dev)
 
-    def to_slots_wide(rows):
+    def to_slots_wide(rows, table):
         part = rows.stop - rows.start
         both = [
             jnp.einsum(
-                "cqn,nkm->mqkc", fields[0, rows], by_part, preferred_element_type=jnp.float32
+                "cqn,nkm->mqkc", fields[0, rows], table, preferred_element_type=jnp.float32
             ).astype(jnp.bfloat16)
             for fields in (prediction_maps, observed_maps)
         ]
         spec = jnp.stack(both, axis=2)
-        return spec.reshape(blocks, slots, lat_dev, 4 * part)
+        spec = spec.reshape(blocks, spec.shape[0] // blocks, lat_dev, 4 * part)
+        return with_layout_constraint(spec, Layout(major_to_minor=(0, 1, 2, 3)))
 
     def narrow_lines(spec, rows):
         part = rows.stop - rows.start
@@ -103,10 +105,10 @@
         grad_spec = grad_spec.reshape(slots, 2, part, blocks, lat_dev).transpose(3, 1, 0, 2, 4)
         return grad_spec.reshape(blocks, 2 * slots, part * lat_dev)
 
-    def to_grid(grad_spec, rows):
+    def to_grid(grad_lat, rows):
         part = rows.stop - rows.start
         grad_grid = lax.dot_general(
-            exchange(grad_spec).reshape(2 * blocks * slots, part * lat_dev),
+            grad_lat.reshape(2 * blocks * slots, part * lat_dev),
             fourier,
             (((0,), (1,)), ((), ())),
             preferred_element_type=jnp.float32,
@@ -133,27 +135,41 @@
         return jnp.einsum("sqj,sql->sjl", lines, table, preferred_element_type=jnp.float32)
 
     half = slots // 2
+    by_half = by_part.reshape(MERIDIAN_POINTS, 2, blocks, 2, half)
     spec_0 = exchange(to_slots(groups[0]))
-    spec_1 = exchange(to_slots_wide(groups[1]))
+    by_half = after(by_half)
+    low_table, high_table = (
+        by_half[:, :, :, side].reshape(MERIDIAN_POINTS, 2, blocks * half) for side in (0, 1)
+    )
+    spec_1 = exchange(to_slots_wide(groups[1], by_part))
     coef_0, partial_0 = analyse(legendre_narrow(spec_0), groups[0])
-    payload_2 = to_slots_wide(groups[2])
+    low_2 = to_slots_wide(groups[2], low_table)
+    high_2 = to_slots_wide(groups[2], high_table)
+    partial_0, low_2, high_2 = lax.optimization_barrier((partial_0, low_2, high_2))
     power_0 = sum_orders(partial_0)
     spec_1 = after(spec_1)
-    low_2 = exchange(payload_2[:, :half])
+    low_2 = exchange(low_2)
     coef_1, partial_1 = analyse(legendre_wide(spec_1, full_table), groups[1])
+    grad_0 = synthesise(coef_0, power_0, groups[0])
+    partial_1, grad_0 = lax.optimization_barrier((partial_1, grad_0))
     power_1 = sum_orders(partial_1)
-    coef_0, coef_1 = after((coef_0, coef_1))
-    high_2 = exchange(payload_2[:, half:])
-    grad_0 = synthesise(coef_0, power_0, groups[0])
+    high_2 = exchange(high_2)
     grad_1 = synthesise(coef_1, power_1, groups[1])
-    result_0 = to_grid(grad_0, groups[0])
+    grad_cosine, grad_sine = lax.optimization_barrier((grad_1[:, :slots], grad_1[:, slots:]))
+    cosine_1 = exchange(grad_cosine)
     spec_2 = jnp.concatenate([low_2, high_2], axis=1)
     coef_2, partial_2 = analyse(legendre_wide(spec_2, full_table), groups[2])
     power_2 = sum_orders(partial_2)
-    coef_2 = after(coef_2)
-    result_1 = to_grid(grad_1, groups[1])
-    result_2 = to_grid(synthesise(coef_2, power_2, groups[2]), groups[2])
-    return jnp.concatenate([result_0, result_1, result_2], axis=0)[None]
+    sine_1 = exchange(grad_sine)
+    grad_2 = synthesise(coef_2, power_2, groups[2])
+    lat_0 = exchange(grad_0)
+    lat_2 = exchange(grad_2)
+    results = [
+        to_grid(lat_0, groups[0]),
+        to_grid(jnp.concatenate([cosine_1, sine_1], axis=1), groups[1]),
+        to_grid(lat_2, groups[2]),
+    ]
+    return jnp.concatenate(results, axis=0)[None]
 
 
 def solution(mesh):

time: 635 us -> 565 us (0.89)
  waiting for transfers between devices: 207 us -> 124 us
  blocking collectives: 20.1 us -> 58.9 us
  local copies, waits for them, and re-layouts: 202 us -> 176 us
  other arithmetic: 25.3 us -> 36.9 us
  starting transfers between devices: 57.6 us -> 46.4 us
    all_to_all x12 -> x9, waiting for transfers between devices: 206 us -> 123 us  [exchange(): lax.all_to_all(array, 'mp', split_axis=0, concat_axis=0, tiled=True)]
    optimization_barrier x4 -> x0, local copies, waits for them, and re-layouts: 39.8 us -> none  [the longest x3 36.1 us: exchange(): array, _ = lax.optimization_barrier((array, last[0]))]
    all_to_all x2 -> x6, blocking collectives: 20.1 us -> 58.9 us  [exchange(): lax.all_to_all(array, 'mp', split_axis=0, concat_axis=0, tiled=True)]
    slice x1 -> x2, local copies, waits for them, and re-layouts: 19.1 us -> 2.51 us  [the longest x1 1.58 us: local(): grad_1[:, slots:]]
    reshape x2 -> x4, local copies, waits for them, and re-layouts: 34.3 us -> 49.2 us  [to_slots_wide(): spec = spec.reshape(blocks, spec.shape[0] // blocks, lat_dev, 4 * part)]
    all_to_all x12 -> x9, starting transfers between devices: 57.6 us -> 46.4 us  [exchange(): lax.all_to_all(array, 'mp', split_axis=0, concat_axis=0, tiled=True)]
    another operation x2, local copies, waits for them, and re-layouts: 6.75 us -> 14.2 us  [to_slots_wide(): spec = jnp.stack(both, axis=2)]
    transpose x0 -> x2, local copies, waits for them, and re-layouts: none -> 7.29 us  [legendre_wide(): spec.transpose(1, 0, 2, 3).reshape(table.shape[0], latitudes, spec.shape[3])]
  transfers between devices with their start and end apart: 13 -> 10, of which waited for: 9 -> 6; matrix products, arithmetic and copies ran while one was open for 39% -> 54% of each run, Pallas kernels for 0% -> 0%
where the time goes in v4:
time: 565 us; the launch traced here: 553 us
  local copies, waits for them, and re-layouts  176 us (31%)
  waiting for transfers between devices  124 us (22%)
  matrix products  96.9 us (17%)
  blocking collectives  58.9 us (10%)
  starting transfers between devices  46.4 us (8%)
  other arithmetic  36.9 us (7%)
  between operations  14.2 us (3%)
    all_to_all x9, waiting for transfers between devices, exchange(): lax.all_to_all(array, 'mp', split_axis=0, concat_axis=0, tiled=True)  123 us
    all_to_all x6, blocking collectives, exchange(): lax.all_to_all(array, 'mp', split_axis=0, concat_axis=0, tiled=True)  58.9 us
    reshape x4, local copies, waits for them, and re-layouts, to_slots_wide(): spec = spec.reshape(blocks, spec.shape[0] // blocks, lat_dev, 4 * part)  49.2 us
    all_to_all x9, starting transfers between devices, exchange(): lax.all_to_all(array, 'mp', split_axis=0, concat_axis=0, tiled=True)  46.4 us
    reshape x6, local copies, waits for them, and re-layouts, synthesise(): grad_spec.reshape(slots, 2, part, blocks, lat_dev).transpose(3, 1, 0, 2, 4)  37 us
    dot_general x3, matrix products, synthesise(): jnp.einsum('sjl,sql->sjq', grad_coef.reshape(slots, 2 * part, degrees), f...  33 us
    reshape x3, local copies, waits for them, and re-layouts, synthesise(): return grad_spec.reshape(blocks, 2 * slots, part * lat_dev)  28 us
    dot_general x2, matrix products, legendre_wide(): jnp.einsum('sqj,sql->sjl', lines, table, preferred_element_type=jnp.float32)  26.2 us
  transfers between devices with their start and end apart: 10, of which 6 were waited for; matrix products, arithmetic and copies ran while one was open for 54% of the time, Pallas kernels for 0%

profile of v4, /device:TPU:0, one launch (start us, length us, event | category | flops | bytes accessed | tf_op | source)
XLA Modules:
  0.0 553.5 jit_solution(17565243281802959397)
XLA Ops:
  7.9 7.3 %all-to-all-start = ((s32[8,1,48]{2,1,0:T(1,128)}), s32[8,1,48]{2,1,0:T(1,128)S(1)}, u32[]{:S(2)}, u32[]{:S(2)}) async-start(s32[8,1,48]{2,1,0:T(1,128)} %broadcast_in_dim.20), calls=%async_computation | async-start | bytes 8192 | tf_op jit(solution)/shard_map/all_to_all | solution.py:35
  16.6 5.0 all-to-all-done
  21.5 5.4 multiply_convert_fusion.3
  27.1 2.1 convolution_convert_fusion.4
  29.2 3.6 all-to-all-start.1
  34.0 5.1 multiply_convert_fusion.5
  39.1 3.7 convert_bitcast_fusion
  42.8 3.7 convert_bitcast_fusion.1
  46.4 2.7 pad_maximum_fusion
  49.2 17.1 %reshape.379 = bf16[8,48,48,128]{1,0,2,3:T(8,128)(2,1)} reshape(bf16[384,48,2,2,32]{0,1,4,3,2:T(8,128)(2,1)} %pad_maximum_fusion) | data formatting | bytes 9437184 | tf_op jit(solution)/shard_map/reshape | solution.py:72
  66.3 18.9 %copy.42 = bf16[8,48,48,128]{3,2,1,0:T(8,128)(2,1)} copy(bf16[8,48,48,128]{1,0,2,3:T(8,128)(2,1)} %reshape.379) | data formatting | bytes 9437184 | tf_op jit(solution)/shard_map/reshape | solution.py:72
  86.2 6.3 %all-to-all-start.2 = ((bf16[8,48,48,128]{3,2,1,0:T(8,128)(2,1)}), bf16[8,48,48,128]{3,2,1,0:T(8,128)(2,1)}, u32[]{:S(2)}, u32[]{:S(2)}) async-start(bf16[8,48,48,128]{3,2,1,0:T(8,128)(2,1)} %copy.42), calls=%async_computation.2 | async-start | bytes 9437184 | tf_op jit(solution)/shard_map/all_to_all | solution.py:35
  92.6 5.4 multiply_convert_fusion.1
  99.1 3.6 fusion.43
  104.8 7.1 %copy.47 = bf16[192,48,2,2,32]{1,4,3,2,0:T(8,128)(2,1)} copy(bf16[192,48,2,2,32]{0,1,4,3,2:T(8,128)(2,1)S(1)} %pad_maximum_fusion.2) | data formatting | bytes 4718592 | tf_op jit(solution)/shard_map/stack | solution.py:71
  111.9 6.6 %copy.48 = bf16[8,24,48,128]{3,2,1,0:T(8,128)(2,1)} copy(bf16[8,24,48,128]{2,3,1,0:T(8,128)(2,1)} %bitcast.215) | data formatting | bytes 4718592 | tf_op jit(solution)/shard_map/reshape | solution.py:72
  118.5 3.1 fusion.46
  121.6 3.1 fusion.52
  125.3 7.1 %copy.45 = bf16[192,48,2,2,32]{1,4,3,2,0:T(8,128)(2,1)} copy(bf16[192,48,2,2,32]{0,1,4,3,2:T(8,128)(2,1)S(1)} %pad_maximum_fusion.1) | data formatting | bytes 4718592 | tf_op jit(solution)/shard_map/stack | solution.py:71
  132.4 6.5 %copy.46 = bf16[8,24,48,128]{3,2,1,0:T(8,128)(2,1)} copy(bf16[8,24,48,128]{2,3,1,0:T(8,128)(2,1)} %bitcast.216) | data formatting | bytes 4718592 | tf_op jit(solution)/shard_map/reshape | solution.py:72
  138.9 5.2 reshape.348
  144.1 5.3 copy.69
  149.4 4.4 reshape.349
  153.8 8.7 %fusion.8 = (f32[32,384]{1,0:T(8,128)S(1)}, f32[48,32,384]{2,1,0:T(8,128)}) fusion(f32[48]{0:T(128)S(1)} %compare_select_fusion, bf16[48,32,384]{2,1,0:T(8,128)(2,1)S(1)} %reshape.349, bf16[48,384,384]{2,1,0:T(8,128)(2,1)} %all-gather.2.cloned.1.call-done), kind=kOutput, calls=%fused_computation.25 | convolution fusion | flops 454742016 | bytes 17744064 | tf_op jit(solution)/shard_map/sjq,sql->sjl/dot_general | solution.py:126
  162.5 32.7 %all-to-all-done.2 = bf16[8,48,48,128]{3,2,1,0:T(8,128)(2,1)} async-done(((bf16[8,48,48,128]{3,2,1,0:T(8,128)(2,1)}), bf16[8,48,48,128]{3,2,1,0:T(8,128)(2,1)}, u32[]{:S(2)}, u32[]{:S(2)}) %all-to-all-start.2) | async-done | bytes 4718624 | tf_op jit(solution)/shard_map/all_to_all | solution.py:35
  195.3 10.1 %all_to_all.75 = f32[8,6,128]{2,1,0:T(8,128)S(1)} all-to-all(f32[8,6,128]{2,1,0:T(8,128)S(1)} %reshape.352), channel_id=1, replica_groups=mesh['dp'=4,'mp'=8] {'mp'}, dimensions={0} | all-to-all | bytes 49152 | tf_op jit(solution)/shard_map/all_to_all | solution.py:35
  205.4 9.1 %all_to_all.76 = f32[8,6,128]{2,1,0:T(8,128)S(1)} all-to-all(f32[8,6,128]{2,1,0:T(8,128)S(1)} %broadcast_in_dim.21), channel_id=1, replica_groups=mesh['dp'=4,'mp'=8] {'mp'}, dimensions={0} | all-to-all | bytes 49152 | tf_op jit(solution)/shard_map/all_to_all | solution.py:35
  214.5 3.8 all-to-all-start.5
  218.3 5.9 %copy.49 = bf16[48,8,48,128]{3,2,1,0:T(8,128)(2,1)} copy(bf16[48,8,48,128]{3,2,0,1:T(8,128)(2,1)} %bitcast.44) | data formatting | bytes 9437184 | tf_op jit(solution)/shard_map/transpose | solution.py:134
  224.3 10.0 %convolution_convert_fusion.6 = bf16[48,16,384]{2,1,0:T(8,128)(2,1)S(1)} fusion(bf16[48,384,384]{2,1,0:T(8,128)(2,1)} %all-gather.2.cloned.1.call-done, f32[48,2,2,8,384]{4,3,2,1,0:T(8,128)} %bitcast.220, f32[16,384]{1,0:T(8,128)S(1)} %broadcast_bitcast_fusion, f32[16,384]{1,0:T(8,128)S(1)} %broadcast_bitcast_fusion.1, f32[48]{0:T(128)S(1)} %compare_select_fusion), kind=kOutput, calls=%fused_computation.63 | convolution fusion | flops 228261888 | bytes 17154240 | tf_op jit(solution)/shard_map/sjl,sql->sjq/dot_general | solution.py:99
  234.3 2.3 reshape.355
  236.6 2.9 copy.70
  239.5 3.2 reshape.356
  242.7 13.8 %fusion = (f32[128,384]{1,0:T(8,128)S(1)}, f32[48,128,384]{2,1,0:T(8,128)}) fusion(f32[48]{0:T(128)S(1)} %compare_select_fusion, bf16[48,384,128]{2,1,0:T(8,128)(2,1)} %bitcast.213, bf16[48,384,384]{2,1,0:T(8,128)(2,1)} %all-gather.2.cloned.1.call-done), kind=kOutput, calls=%fused_computation.2 | convolution fusion | flops 1818968064 | bytes 28508352 | tf_op jit(solution)/shard_map/sqj,sql->sjl/dot_general | solution.py:135
  256.5 13.6 %all-to-all-done.5 = bf16[8,24,48,128]{3,2,1,0:T(8,128)(2,1)S(1)} async-done(((bf16[8,24,48,128]{3,2,1,0:T(8,128)(2,1)}), bf16[8,24,48,128]{3,2,1,0:T(8,128)(2,1)S(1)}, u32[]{:S(2)}, u32[]{:S(2)}) %all-to-all-start.5) | async-done | bytes 2359328 | tf_op jit(solution)/shard_map/all_to_all | solution.py:35
  270.1 10.3 %all_to_all.77 = f32[8,24,128]{2,1,0:T(8,128)S(1)} all-to-all(f32[8,24,128]{2,1,0:T(8,128)S(1)} %reshape.357), channel_id=1, replica_groups=mesh['dp'=4,'mp'=8] {'mp'}, dimensions={0} | all-to-all | bytes 196608 | tf_op jit(solution)/shard_map/all_to_all | solution.py:35
  280.4 9.5 %all_to_all.78 = f32[8,24,128]{2,1,0:T(8,128)S(1)} all-to-all(f32[8,24,128]{2,1,0:T(8,128)S(1)} %broadcast_in_dim.22), channel_id=1, replica_groups=mesh['dp'=4,'mp'=8] {'mp'}, dimensions={0} | all-to-all | bytes 196608 | tf_op jit(solution)/shard_map/all_to_all | solution.py:35
  289.9 4.6 all-to-all-start.8
  294.5 9.3 %fusion.90 = (f32[48,1,2,32,384]{4,3,2,1,0:T(8,128)}, f32[48,1,2,32,384]{4,3,2,1,0:T(8,128)}) fusion(f32[48,2,2,32,384]{4,3,2,1,0:T(8,128)} %bitcast.212), kind=kLoop, calls=%fused_computation.130 | loop fusion | bytes 18874368 | tf_op jit(solution)/shard_map/slice | solution.py:97
  303.9 5.0 fusion.7
  308.9 11.5 %convolution_convert_fusion.3 = bf16[48,64,384]{2,1,0:T(8,128)(2,1)} fusion(bf16[48,64,384]{2,1,0:T(8,128)(2,1)S(1)} %fusion.7, bf16[48,384,384]{2,1,0:T(8,128)(2,1)} %all-gather.2.cloned.1.call-done), kind=kOutput, calls=%fused_computation.48 | convolution fusion | flops 907149312 | bytes 18874368 | tf_op jit(solution)/shard_map/sjl,sql->sjq/dot_general | solution.py:99
  320.4 9.2 %reshape.359 = bf16[48,2,32,8,48]{4,3,2,1,0:T(8,128)(2,1)} reshape(bf16[48,64,384]{2,1,0:T(8,128)(2,1)} %convolution_convert_fusion.3) | data formatting | bytes 4718592 | tf_op jit(solution)/shard_map/reshape | solution.py:105
  329.7 6.6 %copy.68 = bf16[48,2,32,8,48]{4,2,0,1,3:T(8,128)(2,1)} copy(bf16[48,2,32,8,48]{4,3,2,1,0:T(8,128)(2,1)} %reshape.359) | data formatting | bytes 4718592 | tf_op jit(solution)/shard_map/reshape | solution.py:105
  336.3 12.0 %reshape.360 = bf16[8,96,1536]{2,1,0:T(8,128)(2,1)S(1)} reshape(bf16[8,2,48,32,48]{4,3,2,1,0:T(8,128)(2,1)} %bitcast.217) | data formatting | bytes 4718592 | tf_op jit(solution)/shard_map/reshape | solution.py:106
  349.9 6.4 %all-to-all-start.9 = ((bf16[8,48,1536]{2,1,0:T(8,128)(2,1)}), bf16[8,48,1536]{2,1,0:T(8,128)(2,1)S(1)}, u32[]{:S(2)}, u32[]{:S(2)}) async-start(bf16[8,48,1536]{2,1,0:T(8,128)(2,1)} %get-tuple-element.47), calls=%async_computation.9 | async-start | bytes 2359296 | tf_op jit(solution)/shard_map/all_to_all | solution.py:35
  356.3 2.1 maximum_bitcast_fusion.1
  359.7 12.4 %fusion.1 = (f32[128,384]{1,0:T(8,128)S(1)}, f32[48,128,384]{2,1,0:T(8,128)}) fusion(f32[48]{0:T(128)S(1)} %compare_select_fusion, bf16[48,384,128]{2,1,0:T(8,128)(2,1)S(1)} %bitcast.214, bf16[48,384,384]{2,1,0:T(8,128)(2,1)} %all-gather.2.cloned.1.call-done), kind=kOutput, calls=%fused_computation.3 | convolution fusion | flops 1818968064 | bytes 28508352 | tf_op jit(solution)/shard_map/sqj,sql->sjl/dot_general | solution.py:135
  372.2 10.2 %all-to-all-done.9 = bf16[8,48,1536]{2,1,0:T(8,128)(2,1)S(1)} async-done(((bf16[8,48,1536]{2,1,0:T(8,128)(2,1)}), bf16[8,48,1536]{2,1,0:T(8,128)(2,1)S(1)}, u32[]{:S(2)}, u32[]{:S(2)}) %all-to-all-start.9) | async-done | bytes 1179680 | tf_op jit(solution)/shard_map/all_to_all | solution.py:35
  382.4 10.3 %all_to_all.79 = f32[8,24,128]{2,1,0:T(8,128)S(1)} all-to-all(f32[8,24,128]{2,1,0:T(8,128)S(1)} %reshape.362), channel_id=1, replica_groups=mesh['dp'=4,'mp'=8] {'mp'}, dimensions={0} | all-to-all | bytes 196608 | tf_op jit(solution)/shard_map/all_to_all | solution.py:35
  392.7 9.5 %all_to_all.80 = f32[8,24,128]{2,1,0:T(8,128)S(1)} all-to-all(f32[8,24,128]{2,1,0:T(8,128)S(1)} %broadcast_in_dim.23), channel_id=1, replica_groups=mesh['dp'=4,'mp'=8] {'mp'}, dimensions={0} | all-to-all | bytes 196608 | tf_op jit(solution)/shard_map/all_to_all | solution.py:35
  402.2 3.6 all-to-all-start.12
  405.8 9.2 %fusion.91 = (f32[48,1,2,32,384]{4,3,2,1,0:T(8,128)}, f32[48,1,2,32,384]{4,3,2,1,0:T(8,128)}) fusion(f32[48,2,2,32,384]{4,3,2,1,0:T(8,128)} %bitcast.211), kind=kLoop, calls=%fused_computation.131 | loop fusion | bytes 18874368 | tf_op jit(solution)/shard_map/slice | solution.py:97
  416.0 15.7 %all-to-all-done.12 = bf16[8,48,1536]{2,1,0:T(8,128)(2,1)S(1)} async-done(((bf16[8,48,1536]{2,1,0:T(8,128)(2,1)}), bf16[8,48,1536]{2,1,0:T(8,128)(2,1)S(1)}, u32[]{:S(2)}, u32[]{:S(2)}) %all-to-all-start.12) | async-done | bytes 1179680 | tf_op jit(solution)/shard_map/all_to_all | solution.py:35
  431.6 4.7 all-to-all-start.13
  436.4 5.0 fusion.4
  441.4 11.5 %convolution_convert_fusion.2 = bf16[48,64,384]{2,1,0:T(8,128)(2,1)} fusion(bf16[48,64,384]{2,1,0:T(8,128)(2,1)S(1)} %fusion.4, bf16[48,384,384]{2,1,0:T(8,128)(2,1)} %all-gather.2.cloned.1.call-done), kind=kOutput, calls=%fused_computation.47 | convolution fusion | flops 907149312 | bytes 18874368 | tf_op jit(solution)/shard_map/sjl,sql->sjq/dot_general | solution.py:99
  452.9 9.2 %reshape.368 = bf16[48,2,32,8,48]{4,3,2,1,0:T(8,128)(2,1)} reshape(bf16[48,64,384]{2,1,0:T(8,128)(2,1)} %convolution_convert_fusion.2) | data formatting | bytes 4718592 | tf_op jit(solution)/shard_map/reshape | solution.py:105
  462.1 6.7 %copy.67 = bf16[48,2,32,8,48]{4,2,0,1,3:T(8,128)(2,1)} copy(bf16[48,2,32,8,48]{4,3,2,1,0:T(8,128)(2,1)} %reshape.368) | data formatting | bytes 4718592 | tf_op jit(solution)/shard_map/reshape | solution.py:105
  468.8 12.8 %reshape.369 = bf16[8,96,1536]{2,1,0:T(8,128)(2,1)} reshape(bf16[8,2,48,32,48]{4,3,2,1,0:T(8,128)(2,1)} %bitcast.218) | data formatting | bytes 4718592 | tf_op jit(solution)/shard_map/reshape | solution.py:106
  481.6 6.3 %all-to-all-start.14 = ((bf16[8,96,1536]{2,1,0:T(8,128)(2,1)}), bf16[8,96,1536]{2,1,0:T(8,128)(2,1)}, u32[]{:S(2)}, u32[]{:S(2)}) async-start(bf16[8,96,1536]{2,1,0:T(8,128)(2,1)} %reshape.369), calls=%async_computation.14 | async-start | bytes 4718592 | tf_op jit(solution)/shard_map/all_to_all | solution.py:35
  491.3 2.6 convolution_convert_fusion.5
  493.9 46.0 %all-to-all-done.14 = bf16[8,96,1536]{2,1,0:T(8,128)(2,1)} async-done(((bf16[8,96,1536]{2,1,0:T(8,128)(2,1)}), bf16[8,96,1536]{2,1,0:T(8,128)(2,1)}, u32[]{:S(2)}, u32[]{:S(2)}) %all-to-all-start.14) | async-done | bytes 2359328 | tf_op jit(solution)/shard_map/all_to_all | solution.py:35
  539.9 3.8 convolution_convert_fusion
  543.6 2.8 maximum_bitcast_fusion
  (86 shorter events, 16.4 us)
Async XLA Ops:
  6.5 0.7 copy-start.12
  6.5 147.3 %all-gather.2.cloned.1.call-start = ((), (), s32[]{:S(2)}) async-start(), calls=%async_computation.15 | async-start | bytes 17694720 | tf_op jit(solution)/shard_map/all_gather | solution.py:43
  7.9 13.6 %all-to-all-start = ((s32[8,1,48]{2,1,0:T(1,128)}), s32[8,1,48]{2,1,0:T(1,128)S(1)}, u32[]{:S(2)}, u32[]{:S(2)}) async-start(s32[8,1,48]{2,1,0:T(1,128)} %broadcast_in_dim.20), calls=%async_computation | async-start | bytes 8192 | tf_op jit(solution)/shard_map/all_to_all | solution.py:35
  27.0 2.2 copy-start.5
  29.2 56.0 %all-to-all-start.1 = ((bf16[8,96,768]{2,1,0:T(8,128)(2,1)}), bf16[8,96,768]{2,1,0:T(8,128)(2,1)S(1)}, u32[]{:S(2)}, u32[]{:S(2)}) async-start(bf16[8,96,768]{2,1,0:T(8,128)(2,1)} %bitcast.17), calls=%async_computation.1 | async-start | bytes 2359296 | tf_op jit(solution)/shard_map/all_to_all | solution.py:35
  85.2 1.0 copy-start.2
  86.2 109.0 %all-to-all-start.2 = ((bf16[8,48,48,128]{3,2,1,0:T(8,128)(2,1)}), bf16[8,48,48,128]{3,2,1,0:T(8,128)(2,1)}, u32[]{:S(2)}, u32[]{:S(2)}) async-start(bf16[8,48,48,128]{3,2,1,0:T(8,128)(2,1)} %copy.42), calls=%async_computation.2 | async-start | bytes 9437184 | tf_op jit(solution)/shard_map/all_to_all | solution.py:35
  98.2 4.6 slice-start
  99.1 3.6 slice-start.1
  111.9 6.6 %copy-start.8 = (bf16[768,2,8,1,24]{0,4,2,1,3:T(8,128)(2,1)S(1)}, bf16[768,2,8,1,24]{0,4,2,1,3:T(8,128)(2,1)}, u32[]{:S(2)}) copy-start(bf16[768,2,8,1,24]{0,4,2,1,3:T(8,128)(2,1)} %get-tuple-element.60) | copy-start | bytes 1769476
  214.5 55.6 %all-to-all-start.5 = ((bf16[8,24,48,128]{3,2,1,0:T(8,128)(2,1)}), bf16[8,24,48,128]{3,2,1,0:T(8,128)(2,1)S(1)}, u32[]{:S(2)}, u32[]{:S(2)}) async-start(bf16[8,24,48,128]{3,2,1,0:T(8,128)(2,1)} %copy.46), calls=%async_computation.5 | async-start | bytes 4718592 | tf_op jit(solution)/shard_map/all_to_all | solution.py:35
  218.3 6.0 %copy-start.10 = (f32[384,72]{0,1:T(8,128)S(1)}, f32[384,72]{0,1:T(8,128)}, u32[]{:S(2)}) copy-start(f32[384,72]{0,1:T(8,128)} %param.10) | copy-start | bytes 331780
  218.3 6.0 %copy-start.11 = (f32[384,72]{0,1:T(8,128)S(1)}, f32[384,72]{0,1:T(8,128)}, u32[]{:S(2)}) copy-start(f32[384,72]{0,1:T(8,128)} %param.11) | copy-start | bytes 331780
  270.1 19.9 %copy-start = (bf16[8,24,48,128]{3,2,1,0:T(8,128)(2,1)}, bf16[8,24,48,128]{3,2,1,0:T(8,128)(2,1)S(1)}, u32[]{:S(2)}) copy-start(bf16[8,24,48,128]{3,2,1,0:T(8,128)(2,1)S(1)} %all-to-all-done.5) | copy-start | bytes 7077892
  289.9 60.0 %all-to-all-start.8 = ((bf16[8,24,48,128]{3,2,1,0:T(8,128)(2,1)}), bf16[8,24,48,128]{3,2,1,0:T(8,128)(2,1)}, u32[]{:S(2)}, u32[]{:S(2)}) async-start(bf16[8,24,48,128]{3,2,1,0:T(8,128)(2,1)} %copy.48), calls=%async_computation.8 | async-start | bytes 4718592 | tf_op jit(solution)/shard_map/all_to_all | solution.py:35
  349.9 6.4 %copy-start.1 = (bf16[8,24,48,128]{3,2,1,0:T(8,128)(2,1)S(1)}, bf16[8,24,48,128]{3,2,1,0:T(8,128)(2,1)}, u32[]{:S(2)}) copy-start(bf16[8,24,48,128]{3,2,1,0:T(8,128)(2,1)} %copy-done) | copy-start | bytes 7077892
  349.9 32.5 %all-to-all-start.9 = ((bf16[8,48,1536]{2,1,0:T(8,128)(2,1)}), bf16[8,48,1536]{2,1,0:T(8,128)(2,1)S(1)}, u32[]{:S(2)}, u32[]{:S(2)}) async-start(bf16[8,48,1536]{2,1,0:T(8,128)(2,1)} %get-tuple-element.47), calls=%async_computation.9 | async-start | bytes 2359296 | tf_op jit(solution)/shard_map/all_to_all | solution.py:35
  402.2 29.4 %all-to-all-start.12 = ((bf16[8,48,1536]{2,1,0:T(8,128)(2,1)}), bf16[8,48,1536]{2,1,0:T(8,128)(2,1)S(1)}, u32[]{:S(2)}, u32[]{:S(2)}) async-start(bf16[8,48,1536]{2,1,0:T(8,128)(2,1)} %get-tuple-element.50), calls=%async_computation.12 | async-start | bytes 2359296 | tf_op jit(solution)/shard_map/all_to_all | solution.py:35
  431.6 4.7 copy-start.3
  431.6 49.9 %all-to-all-start.13 = ((bf16[8,96,384]{2,1,0:T(8,128)(2,1)}), bf16[8,96,384]{2,1,0:T(8,128)(2,1)}, u32[]{:S(2)}, u32[]{:S(2)}) async-start(bf16[8,96,384]{2,1,0:T(8,128)(2,1)} %reshape.356), calls=%async_computation.13 | async-start | bytes 1179648 | tf_op jit(solution)/shard_map/all_to_all | solution.py:35
  481.6 6.3 %copy-start.4 = (bf16[8,48,1536]{2,1,0:T(8,128)(2,1)S(1)}, bf16[8,48,1536]{2,1,0:T(8,128)(2,1)}, u32[]{:S(2)}) copy-start(bf16[8,48,1536]{2,1,0:T(8,128)(2,1)} %copy-done.3) | copy-start | bytes 3538948
  481.6 58.3 %all-to-all-start.14 = ((bf16[8,96,1536]{2,1,0:T(8,128)(2,1)}), bf16[8,96,1536]{2,1,0:T(8,128)(2,1)}, u32[]{:S(2)}, u32[]{:S(2)}) async-start(bf16[8,96,1536]{2,1,0:T(8,128)(2,1)} %reshape.369), calls=%async_computation.14 | async-start | bytes 4718592 | tf_op jit(solution)/shard_map/all_to_all | solution.py:35
  487.9 1.3 copy-start.6
  491.2 48.6 %copy-start.7 = (bf16[768,2,8,48]{0,3,1,2:T(8,128)(2,1)S(1)}, bf16[768,2,8,48]{0,3,1,2:T(8,128)(2,1)}, u32[]{:S(2)}) copy-start(bf16[768,2,8,48]{0,3,1,2:T(8,128)(2,1)} %copy-done.5) | copy-start | bytes 3538948
  539.9 3.8 copy-start.9
Sparse Core Ops, SparseCore 0:
  8.9 93.7 all-gather.1
